TPU v7x, 32 devices: a whole 2x2x4 slice. The times are simulated.
32 devices in a mesh: layer: 4 (over y, x), node: 8 (over z, core).
Axes of the slice: x: 2, y: 2, z: 4, core: 2. Of those that a mesh axis runs over, the one named last changes fastest.
Arguments:
- features: bfloat16 [4, 2048, 512], P(None, 'node'), may hold values from -6 to 6
- w_self: bfloat16 [4, 512, 512], P('layer'), may hold values from -0.1875 to 0.1875
- w_neigh: bfloat16 [4, 512, 512], P('layer'), may hold values from -0.1875 to 0.1875
- w_out: bfloat16 [512, 172], replicated, may hold values from -0.25 to 0.25
- labels: int32 [4, 2048], P(None, 'node'), may hold values from 0 to 171
- train_mask: int32 [4, 2048], P(None, 'node'), may hold values 0 or 1
- tile_cols: int32 [4, 8, 2, 4], P(None, 'node'), may hold values from 0 to 2
- tile_vals: bfloat16 [4, 8, 2, 4, 128, 128], P(None, 'node'), may hold values from -0.25 to 0.25
- send_rows: int32 [4, 8, 8, 8], P(None, 'node'), may hold values from 0 to 255
- send_counts: int32 [4, 8, 8], P(None, 'node'), may hold values from 0 to 8, as said below
Outputs:
- layer_acts: bfloat16 [4, 4, 2048, 512], P('layer', None, 'node')
- act_grads: bfloat16 [4, 4, 2048, 512], P('layer', None, 'node')
- grad_self: float32 [4, 512, 512], P('layer')
- grad_neigh: float32 [4, 512, 512], P('layer')
Inputs may be any that keep to these rules, and one draw needn't show every extreme that they name: `send_counts`: in every span one partition, drawn per span, gets 8 rows from every partition, itself included; the other counts are at most 4. `send_rows`: entries of slots at or past the count are ignored; rows may repeat. `tile_cols`: A value below 2 is a tile of the partition's own rows; larger values are tiles of the received rows in source order, 8 slots per source, then zero rows; tiles of a row tile may repeat.
All inputs are finite; a program needn't handle non-finite values. No bound on the sum of `train_mask` on one device may be relied on, other than what follows from the above.
Results may differ from a plain program's by a relative error of at most 0.03.
Values may be sent and summed in bfloat16 or wider, within the bound.
A program may use at most 128 MiB of HBM per device.

v0:
```python
import jax
import jax.numpy as jnp
from jax import lax
from jax.sharding import PartitionSpec as P


def from_behind(value, axis, steps):
    count = lax.axis_size(axis)
    first, last = (max(0, -steps), min(count, count - steps))
    return lax.ppermute(value, axis, [(source, source + steps) for source in range(first, last)])


def silu_slope(preact):
    sigma = jax.nn.sigmoid(preact)
    return sigma * (1.0 + preact * (1.0 - sigma))


def pick(array, index):
    return lax.dynamic_index_in_dim(array, index, 0, keepdims=False)


def put_row(buffer, value, index, valid):
    current = pick(buffer, index)
    return lax.dynamic_update_index_in_dim(buffer, jnp.where(valid, value, current), index, 0)


def live_slots(send_list, counts):
    return jnp.arange(send_list.shape[1])[None, :] < counts[:, None]


def layer_forward(hidden_in, weight_self, weight_neigh, col_tiles, values, send_list, counts):
    feat_dim = hidden_in.shape[1]
    tile_size = values.shape[-1]
    is_live = live_slots(send_list, counts)
    outgoing = jnp.where(
        is_live[:, :, None], jnp.take(hidden_in, send_list, axis=0), jnp.zeros((), hidden_in.dtype)
    )
    arrived = lax.all_to_all(outgoing, "node", split_axis=0, concat_axis=0, tiled=True)
    extended = jnp.concatenate([hidden_in, arrived.reshape(-1, feat_dim)], axis=0)
    ext_len = extended.shape[0]
    padded_len = (ext_len + tile_size - 1) // tile_size * tile_size
    extended = jnp.pad(extended, ((0, padded_len - ext_len), (0, 0)))
    blocks = jnp.take(extended.reshape(-1, tile_size, feat_dim), col_tiles, axis=0)
    summed = jnp.einsum("rkij,rkjd->rid", values, blocks, preferred_element_type=jnp.float32)
    aggregate = summed.reshape(hidden_in.shape).astype(jnp.bfloat16)
    preact = jnp.dot(hidden_in, weight_self, preferred_element_type=jnp.float32)
    preact = preact + jnp.dot(aggregate, weight_neigh, preferred_element_type=jnp.float32)
    return (aggregate, preact, jax.nn.silu(preact).astype(jnp.bfloat16))


def layer_backward(
    d_out,
    hidden_in,
    aggregate,
    preact,
    weight_self,
    weight_neigh,
    col_tiles,
    values,
    send_list,
    counts,
):
    node_rows, feat_dim = hidden_in.shape
    row_tiles, degree, tile_size = (values.shape[0], values.shape[1], values.shape[-1])
    peers, slot_count = send_list.shape
    d_pre = (d_out.astype(jnp.float32) * silu_slope(preact)).astype(jnp.bfloat16)
    over_rows = (((0,), (0,)), ((), ()))
    over_cols = (((1,), (1,)), ((), ()))
    g_self = lax.dot_general(hidden_in, d_pre, over_rows, preferred_element_type=jnp.float32)
    g_neigh = lax.dot_general(aggregate, d_pre, over_rows, preferred_element_type=jnp.float32)
    back_self = lax.dot_general(d_pre, weight_self, over_cols, preferred_element_type=jnp.float32)
    d_agg = lax.dot_general(
        d_pre, weight_neigh, over_cols, preferred_element_type=jnp.float32
    ).astype(jnp.bfloat16)
    pieces = jnp.einsum(
        "rkij,rid->rkjd",
        values,
        d_agg.reshape(row_tiles, tile_size, feat_dim),
        preferred_element_type=jnp.float32,
    )
    col_count = (node_rows + peers * slot_count + tile_size - 1) // tile_size
    selector = (col_tiles.reshape(-1)[None, :] == jnp.arange(col_count)[:, None]).astype(
        jnp.float32
    )
    d_ext = jnp.einsum(
        "cn,njd->cjd",
        selector,
        pieces.reshape(row_tiles * degree, tile_size, feat_dim),
        precision=lax.Precision.HIGHEST,
    )
    d_ext = d_ext.reshape(-1, feat_dim)
    local_part = d_ext[:node_rows]
    remote = (
        d_ext[node_rows : node_rows + peers * slot_count]
        .reshape(peers, slot_count, feat_dim)
        .astype(jnp.bfloat16)
    )
    returned = lax.all_to_all(remote, "node", split_axis=0, concat_axis=0, tiled=True)
    is_live = live_slots(send_list, counts)
    masked = jnp.where(
        is_live[:, :, None], returned.astype(jnp.float32), jnp.zeros((), jnp.float32)
    )
    scattered = jax.ops.segment_sum(
        masked.reshape(-1, feat_dim), send_list.reshape(-1), num_segments=node_rows
    )
    d_in = (back_self + local_part + scattered).astype(jnp.bfloat16)
    return (d_in, g_self, g_neigh)


def finish_grads(grad_pair, scale):
    summed = (
        lax.psum(grad_pair[0].astype(jnp.bfloat16), "node").astype(jnp.float32),
        lax.psum(grad_pair[1].astype(jnp.bfloat16), "node").astype(jnp.float32),
    )
    return (summed[0] * scale, summed[1] * scale)


def body(
    features,
    w_self,
    w_neigh,
    w_out,
    labels,
    train_mask,
    tile_cols,
    tile_vals,
    send_rows,
    send_counts,
):
    my_section = lax.axis_index("layer")
    sections = lax.axis_size("layer")
    spans, node_rows, feat_dim = features.shape
    classes = w_out.shape[1]
    scale = 1.0 / (spans * node_rows * lax.axis_size("node"))

    def graph_of(span_idx):
        return (
            pick(tile_cols, span_idx)[0],
            pick(tile_vals, span_idx)[0],
            pick(send_rows, span_idx)[0],
            pick(send_counts, span_idx)[0],
        )

    rows_zero = jnp.zeros((node_rows, feat_dim), jnp.bfloat16)
    block_bf = jnp.zeros((spans, node_rows, feat_dim), jnp.bfloat16)
    block_f32 = jnp.zeros((spans, node_rows, feat_dim), jnp.float32)
    square_zero = jnp.zeros((feat_dim, feat_dim), jnp.float32)
    weight_self = w_self[0]
    weight_neigh = w_neigh[0]
    steps_total = spans + sections - 1

    def forward_step(step, carry):
        incoming, saved_in, saved_agg, saved_pre, acts = carry
        span_idx = step - my_section
        valid = (span_idx >= 0) & (span_idx < spans)
        safe_idx = jnp.clip(span_idx, 0, spans - 1)
        hidden_in = jnp.where(my_section == 0, pick(features, safe_idx), incoming)
        aggregate, preact, hidden_out = layer_forward(
            hidden_in, weight_self, weight_neigh, *graph_of(safe_idx)
        )
        saved_in = put_row(saved_in, hidden_in, safe_idx, valid)
        saved_agg = put_row(saved_agg, aggregate, safe_idx, valid)
        saved_pre = put_row(saved_pre, preact, safe_idx, valid)
        acts = put_row(acts, hidden_out, safe_idx, valid)
        outgoing = from_behind(hidden_out, "layer", 1)
        return (outgoing, saved_in, saved_agg, saved_pre, acts)

    start = (rows_zero, block_bf, block_bf, block_f32, block_bf)
    fwd_done = lax.fori_loop(0, steps_total, forward_step, start)
    saved_in, saved_agg, saved_pre, acts = (fwd_done[1], fwd_done[2], fwd_done[3], fwd_done[4])
    logits = jnp.einsum("...d,dc->...c", acts, w_out, preferred_element_type=jnp.float32)
    expo = jnp.exp(logits)
    probs = expo / jnp.sum(expo, axis=-1, keepdims=True)
    onehot = (labels[..., None] == jnp.arange(classes)).astype(jnp.float32)
    g_logits = (train_mask[..., None].astype(jnp.float32) * (probs - onehot)).astype(jnp.bfloat16)
    d_top = jnp.einsum("...c,dc->...d", g_logits, w_out, preferred_element_type=jnp.float32).astype(
        jnp.bfloat16
    )

    def backward_step(step, carry):
        incoming, sum_self, sum_neigh, grads_out = carry
        span_idx = step - (sections - 1 - my_section)
        valid = (span_idx >= 0) & (span_idx < spans)
        safe_idx = jnp.clip(span_idx, 0, spans - 1)
        d_out = jnp.where(my_section == sections - 1, pick(d_top, safe_idx), incoming)
        hidden_in = pick(saved_in, safe_idx)
        graph = graph_of(safe_idx)
        aggregate = pick(saved_agg, safe_idx)
        preact = pick(saved_pre, safe_idx)
        d_in, g_self, g_neigh = layer_backward(
            d_out, hidden_in, aggregate, preact, weight_self, weight_neigh, *graph
        )
        sum_self = sum_self + jnp.where(valid, g_self, 0.0)
        sum_neigh = sum_neigh + jnp.where(valid, g_neigh, 0.0)
        grads_out = put_row(grads_out, d_in, safe_idx, valid)
        outgoing = from_behind(d_in, "layer", -1)
        return (outgoing, sum_self, sum_neigh, grads_out)

    bwd_done = lax.fori_loop(
        0, steps_total, backward_step, (rows_zero, square_zero, square_zero, block_bf)
    )
    grad_self, grad_neigh = finish_grads((bwd_done[1][None], bwd_done[2][None]), scale)
    return (acts[None], bwd_done[3][None], grad_self, grad_neigh)


def solution(mesh):
    in_specs = (
        P(None, "node", None),
        P("layer", None, None),
        P("layer", None, None),
        P(),
        P(None, "node"),
        P(None, "node"),
        P(None, "node", None, None),
        P(None, "node", None, None, None, None),
        P(None, "node", None, None),
        P(None, "node", None),
    )
    out_specs = (
        P("layer", None, "node", None),
        P("layer", None, "node", None),
        P("layer", None, None),
        P("layer", None, None),
    )
    return jax.shard_map(body, mesh=mesh, in_specs=in_specs, out_specs=out_specs, check_vma=False)
```

profile of v0, /device:TPU:25, one launch (start us, length us, event | category | flops | bytes accessed | tf_op | source)
XLA Modules:
  0.0 496.4 jit_solution(6621798975289470011)
XLA Ops:
  13.5 204.8 %while.45 = (s32[]{:T(128)}, bf16[256,512]{1,0:T(8,128)(2,1)}, bf16[4,256,512]{2,1,0:T(8,128)(2,1)}, bf16[4,256,512]{2,1,0:T(8,128)(2,1)}, f32[4,256,512]{2,1,0:...) while((s32[]{:T(128)}, bf16[256,512]{1,0:T(8,128)(2,1)}, ...), condition=%wide.region_1.2_spmd, body=%wide.region_0.1_spmd.sunk | while | flops 406194880 | bytes 18754796 | solution.py:169
  45.9 5.9 %all-to-all-start = ((bf16[8,8,512]{2,1,0:T(8,128)(2,1)}), bf16[8,8,512]{2,1,0:T(8,128)(2,1)S(1)}, u32[]{:S(2)}, u32[]{:S(2)}) async-start(bf16[8,8,512]{2,1,0:T(8,128)(2,1)} %fusion.108), calls=%async_computation | async-start | bytes 131072 | tf_op jit(solution)/shard_map/while/body/eval_jaxpr/all_to_all | solution.py:38
  74.9 5.9 %all-to-all-start = ((bf16[8,8,512]{2,1,0:T(8,128)(2,1)}), bf16[8,8,512]{2,1,0:T(8,128)(2,1)S(1)}, u32[]{:S(2)}, u32[]{:S(2)}) async-start(bf16[8,8,512]{2,1,0:T(8,128)(2,1)} %fusion.108), calls=%async_computation | async-start | bytes 131072 | tf_op jit(solution)/shard_map/while/body/eval_jaxpr/all_to_all | solution.py:38
  103.9 5.9 %all-to-all-start = ((bf16[8,8,512]{2,1,0:T(8,128)(2,1)}), bf16[8,8,512]{2,1,0:T(8,128)(2,1)S(1)}, u32[]{:S(2)}, u32[]{:S(2)}) async-start(bf16[8,8,512]{2,1,0:T(8,128)(2,1)} %fusion.108), calls=%async_computation | async-start | bytes 131072 | tf_op jit(solution)/shard_map/while/body/eval_jaxpr/all_to_all | solution.py:38
  118.3 5.7 %collective-permute-start = (bf16[256,512]{1,0:T(8,128)(2,1)S(1)}, bf16[256,512]{1,0:T(8,128)(2,1)}, u32[]{:S(2)}, u32[]{:S(2)}) collective-permute-start(bf16[256,512]{1,0:T(8,128)(2,1)S(1)} %get-tuple-element.1074), channel_id=1, source_target_pairs={{0,8},{8,16},{16,24},{1,9},{9,17},{17,25},{2,10},{10,18},{18,26},{... | collective-permute-start | bytes 786440 | tf_op jit(solution)/shard_map/while/body/eval_jaxpr/ppermute | solution.py:10
  133.6 5.9 %all-to-all-start = ((bf16[8,8,512]{2,1,0:T(8,128)(2,1)}), bf16[8,8,512]{2,1,0:T(8,128)(2,1)S(1)}, u32[]{:S(2)}, u32[]{:S(2)}) async-start(bf16[8,8,512]{2,1,0:T(8,128)(2,1)} %fusion.108), calls=%async_computation | async-start | bytes 131072 | tf_op jit(solution)/shard_map/while/body/eval_jaxpr/all_to_all | solution.py:38
  148.0 5.9 %collective-permute-start = (bf16[256,512]{1,0:T(8,128)(2,1)S(1)}, bf16[256,512]{1,0:T(8,128)(2,1)}, u32[]{:S(2)}, u32[]{:S(2)}) collective-permute-start(bf16[256,512]{1,0:T(8,128)(2,1)S(1)} %get-tuple-element.1074), channel_id=1, source_target_pairs={{0,8},{8,16},{16,24},{1,9},{9,17},{17,25},{2,10},{10,18},{18,26},{... | collective-permute-start | bytes 786440 | tf_op jit(solution)/shard_map/while/body/eval_jaxpr/ppermute | solution.py:10
  163.5 5.9 %all-to-all-start = ((bf16[8,8,512]{2,1,0:T(8,128)(2,1)}), bf16[8,8,512]{2,1,0:T(8,128)(2,1)S(1)}, u32[]{:S(2)}, u32[]{:S(2)}) async-start(bf16[8,8,512]{2,1,0:T(8,128)(2,1)} %fusion.108), calls=%async_computation | async-start | bytes 131072 | tf_op jit(solution)/shard_map/while/body/eval_jaxpr/all_to_all | solution.py:38
  177.9 5.9 %collective-permute-start = (bf16[256,512]{1,0:T(8,128)(2,1)S(1)}, bf16[256,512]{1,0:T(8,128)(2,1)}, u32[]{:S(2)}, u32[]{:S(2)}) collective-permute-start(bf16[256,512]{1,0:T(8,128)(2,1)S(1)} %get-tuple-element.1074), channel_id=1, source_target_pairs={{0,8},{8,16},{16,24},{1,9},{9,17},{17,25},{2,10},{10,18},{18,26},{... | collective-permute-start | bytes 786440 | tf_op jit(solution)/shard_map/while/body/eval_jaxpr/ppermute | solution.py:10
  193.4 5.9 %all-to-all-start = ((bf16[8,8,512]{2,1,0:T(8,128)(2,1)}), bf16[8,8,512]{2,1,0:T(8,128)(2,1)S(1)}, u32[]{:S(2)}, u32[]{:S(2)}) async-start(bf16[8,8,512]{2,1,0:T(8,128)(2,1)} %fusion.108), calls=%async_computation | async-start | bytes 131072 | tf_op jit(solution)/shard_map/while/body/eval_jaxpr/all_to_all | solution.py:38
  207.8 5.9 %collective-permute-start = (bf16[256,512]{1,0:T(8,128)(2,1)S(1)}, bf16[256,512]{1,0:T(8,128)(2,1)}, u32[]{:S(2)}, u32[]{:S(2)}) collective-permute-start(bf16[256,512]{1,0:T(8,128)(2,1)S(1)} %get-tuple-element.1074), channel_id=1, source_target_pairs={{0,8},{8,16},{16,24},{1,9},{9,17},{17,25},{2,10},{10,18},{18,26},{... | collective-permute-start | bytes 786440 | tf_op jit(solution)/shard_map/while/body/eval_jaxpr/ppermute | solution.py:10
  223.3 201.9 %while.46 = (s32[]{:T(128)}, bf16[256,512]{1,0:T(8,128)(2,1)S(1)}, f32[512,512]{1,0:T(8,128)S(1)}, f32[512,512]{1,0:T(8,128)}, bf16[4,256,512]{2,1,0:T(8,128)(2,...) while((s32[]{:T(128)}, bf16[256,512]{1,0:T(8,128)(2,1)S(1)}, ...), condition=%wide.region_5.6_spmd.clone, body=%wide.region_3.5_spmd.clone.sunk | while | flops 693796992 | bytes 26217204 | solution.py:199
  229.6 5.9 %all-to-all-start.1 = ((bf16[8,8,512]{2,1,0:T(8,128)(2,1)}), bf16[8,8,512]{2,1,0:T(8,128)(2,1)S(1)}, u32[]{:S(2)}, u32[]{:S(2)}) async-start(bf16[8,8,512]{2,1,0:T(8,128)(2,1)} %slice_bitcast_fusion.2), calls=%async_computation.1 | async-start | bytes 131072 | tf_op jit(solution)/shard_map/while/body/eval_jaxpr/all_to_all | solution.py:98
  245.1 7.9 %collective-permute-done.1 = bf16[256,512]{1,0:T(8,128)(2,1)S(1)} collective-permute-done((bf16[256,512]{1,0:T(8,128)(2,1)S(1)}, bf16[256,512]{1,0:T(8,128)(2,1)S(1)}, u32[]{:S(2)}, u32[]{:S(2)}) %collective-permute-start.1) | collective-permute-done | bytes 262176 | tf_op jit(solution)/shard_map/while/body/eval_jaxpr/ppermute | solution.py:10
  259.3 5.6 %all-to-all-start.1 = ((bf16[8,8,512]{2,1,0:T(8,128)(2,1)}), bf16[8,8,512]{2,1,0:T(8,128)(2,1)S(1)}, u32[]{:S(2)}, u32[]{:S(2)}) async-start(bf16[8,8,512]{2,1,0:T(8,128)(2,1)} %slice_bitcast_fusion.2), calls=%async_computation.1 | async-start | bytes 131072 | tf_op jit(solution)/shard_map/while/body/eval_jaxpr/all_to_all | solution.py:98
  274.9 7.6 %collective-permute-done.1 = bf16[256,512]{1,0:T(8,128)(2,1)S(1)} collective-permute-done((bf16[256,512]{1,0:T(8,128)(2,1)S(1)}, bf16[256,512]{1,0:T(8,128)(2,1)S(1)}, u32[]{:S(2)}, u32[]{:S(2)}) %collective-permute-start.1) | collective-permute-done | bytes 262176 | tf_op jit(solution)/shard_map/while/body/eval_jaxpr/ppermute | solution.py:10
  304.2 6.7 %collective-permute-done.1 = bf16[256,512]{1,0:T(8,128)(2,1)S(1)} collective-permute-done((bf16[256,512]{1,0:T(8,128)(2,1)S(1)}, bf16[256,512]{1,0:T(8,128)(2,1)S(1)}, u32[]{:S(2)}, u32[]{:S(2)}) %collective-permute-start.1) | collective-permute-done | bytes 262176 | tf_op jit(solution)/shard_map/while/body/eval_jaxpr/ppermute | solution.py:10
  317.3 5.6 %all-to-all-start.1 = ((bf16[8,8,512]{2,1,0:T(8,128)(2,1)}), bf16[8,8,512]{2,1,0:T(8,128)(2,1)S(1)}, u32[]{:S(2)}, u32[]{:S(2)}) async-start(bf16[8,8,512]{2,1,0:T(8,128)(2,1)} %slice_bitcast_fusion.2), calls=%async_computation.1 | async-start | bytes 131072 | tf_op jit(solution)/shard_map/while/body/eval_jaxpr/all_to_all | solution.py:98
  332.8 6.7 %collective-permute-done.1 = bf16[256,512]{1,0:T(8,128)(2,1)S(1)} collective-permute-done((bf16[256,512]{1,0:T(8,128)(2,1)S(1)}, bf16[256,512]{1,0:T(8,128)(2,1)S(1)}, u32[]{:S(2)}, u32[]{:S(2)}) %collective-permute-start.1) | collective-permute-done | bytes 262176 | tf_op jit(solution)/shard_map/while/body/eval_jaxpr/ppermute | solution.py:10
  361.3 6.7 %collective-permute-done.1 = bf16[256,512]{1,0:T(8,128)(2,1)S(1)} collective-permute-done((bf16[256,512]{1,0:T(8,128)(2,1)S(1)}, bf16[256,512]{1,0:T(8,128)(2,1)S(1)}, u32[]{:S(2)}, u32[]{:S(2)}) %collective-permute-start.1) | collective-permute-done | bytes 262176 | tf_op jit(solution)/shard_map/while/body/eval_jaxpr/ppermute | solution.py:10
  389.9 6.7 %collective-permute-done.1 = bf16[256,512]{1,0:T(8,128)(2,1)S(1)} collective-permute-done((bf16[256,512]{1,0:T(8,128)(2,1)S(1)}, bf16[256,512]{1,0:T(8,128)(2,1)S(1)}, u32[]{:S(2)}, u32[]{:S(2)}) %collective-permute-start.1) | collective-permute-done | bytes 262176 | tf_op jit(solution)/shard_map/while/body/eval_jaxpr/ppermute | solution.py:10
  402.9 5.6 %all-to-all-start.1 = ((bf16[8,8,512]{2,1,0:T(8,128)(2,1)}), bf16[8,8,512]{2,1,0:T(8,128)(2,1)S(1)}, u32[]{:S(2)}, u32[]{:S(2)}) async-start(bf16[8,8,512]{2,1,0:T(8,128)(2,1)} %slice_bitcast_fusion.2), calls=%async_computation.1 | async-start | bytes 131072 | tf_op jit(solution)/shard_map/while/body/eval_jaxpr/all_to_all | solution.py:98
  418.4 6.7 %collective-permute-done.1 = bf16[256,512]{1,0:T(8,128)(2,1)S(1)} collective-permute-done((bf16[256,512]{1,0:T(8,128)(2,1)S(1)}, bf16[256,512]{1,0:T(8,128)(2,1)S(1)}, u32[]{:S(2)}, u32[]{:S(2)}) %collective-permute-start.1) | collective-permute-done | bytes 262176 | tf_op jit(solution)/shard_map/while/body/eval_jaxpr/ppermute | solution.py:10
  427.5 57.7 %all-reduce.4.cloned.1.call-done = (bf16[1,512,512]{2,1,0:T(8,128)(2,1)}, bf16[1,512,512]{2,1,0:T(8,128)(2,1)}) async-done(((bf16[1,512,512]{2,1,0:T(8,128)(2,1)}, bf16[1,512,512]{2,1,0:T(8,128)(2,1)}), (bf16[1,512,512]{2,1,0:T(8,128)(2,1)}, bf16[1,512,512]{2,1,0:T(8,128)(2,1)})) %all-reduce.4.cloned.1.call-update) | async-done | bytes 1048592 | tf_op jit(solution)/shard_map/psum | solution.py:112
  (412 shorter events, 292.4 us)
Async XLA Ops:
  7.2 478.0 %all-reduce.4.cloned.1.call-start = ((), (), s32[]{:S(2)}) async-start(), calls=%async_computation.2 | async-start | bytes 2097152 | tf_op jit(solution)/shard_map/psum | solution.py:112
  45.9 9.9 %all-to-all-start = ((bf16[8,8,512]{2,1,0:T(8,128)(2,1)}), bf16[8,8,512]{2,1,0:T(8,128)(2,1)S(1)}, u32[]{:S(2)}, u32[]{:S(2)}) async-start(bf16[8,8,512]{2,1,0:T(8,128)(2,1)} %fusion.108), calls=%async_computation | async-start | bytes 131072 | tf_op jit(solution)/shard_map/while/body/eval_jaxpr/all_to_all | solution.py:38
  60.3 9.6 %collective-permute-start = (bf16[256,512]{1,0:T(8,128)(2,1)S(1)}, bf16[256,512]{1,0:T(8,128)(2,1)}, u32[]{:S(2)}, u32[]{:S(2)}) collective-permute-start(bf16[256,512]{1,0:T(8,128)(2,1)S(1)} %get-tuple-element.1074), channel_id=1, source_target_pairs={{0,8},{8,16},{16,24},{1,9},{9,17},{17,25},{2,10},{10,18},{18,26},{... | collective-permute-start | bytes 786440 | tf_op jit(solution)/shard_map/while/body/eval_jaxpr/ppermute | solution.py:10
  74.9 9.9 %all-to-all-start = ((bf16[8,8,512]{2,1,0:T(8,128)(2,1)}), bf16[8,8,512]{2,1,0:T(8,128)(2,1)S(1)}, u32[]{:S(2)}, u32[]{:S(2)}) async-start(bf16[8,8,512]{2,1,0:T(8,128)(2,1)} %fusion.108), calls=%async_computation | async-start | bytes 131072 | tf_op jit(solution)/shard_map/while/body/eval_jaxpr/all_to_all | solution.py:38
  89.3 9.6 %collective-permute-start = (bf16[256,512]{1,0:T(8,128)(2,1)S(1)}, bf16[256,512]{1,0:T(8,128)(2,1)}, u32[]{:S(2)}, u32[]{:S(2)}) collective-permute-start(bf16[256,512]{1,0:T(8,128)(2,1)S(1)} %get-tuple-element.1074), channel_id=1, source_target_pairs={{0,8},{8,16},{16,24},{1,9},{9,17},{17,25},{2,10},{10,18},{18,26},{... | collective-permute-start | bytes 786440 | tf_op jit(solution)/shard_map/while/body/eval_jaxpr/ppermute | solution.py:10
  103.9 9.9 %all-to-all-start = ((bf16[8,8,512]{2,1,0:T(8,128)(2,1)}), bf16[8,8,512]{2,1,0:T(8,128)(2,1)S(1)}, u32[]{:S(2)}, u32[]{:S(2)}) async-start(bf16[8,8,512]{2,1,0:T(8,128)(2,1)} %fusion.108), calls=%async_computation | async-start | bytes 131072 | tf_op jit(solution)/shard_map/while/body/eval_jaxpr/all_to_all | solution.py:38
  118.3 10.3 %collective-permute-start = (bf16[256,512]{1,0:T(8,128)(2,1)S(1)}, bf16[256,512]{1,0:T(8,128)(2,1)}, u32[]{:S(2)}, u32[]{:S(2)}) collective-permute-start(bf16[256,512]{1,0:T(8,128)(2,1)S(1)} %get-tuple-element.1074), channel_id=1, source_target_pairs={{0,8},{8,16},{16,24},{1,9},{9,17},{17,25},{2,10},{10,18},{18,26},{... | collective-permute-start | bytes 786440 | tf_op jit(solution)/shard_map/while/body/eval_jaxpr/ppermute | solution.py:10
  133.6 9.9 %all-to-all-start = ((bf16[8,8,512]{2,1,0:T(8,128)(2,1)}), bf16[8,8,512]{2,1,0:T(8,128)(2,1)S(1)}, u32[]{:S(2)}, u32[]{:S(2)}) async-start(bf16[8,8,512]{2,1,0:T(8,128)(2,1)} %fusion.108), calls=%async_computation | async-start | bytes 131072 | tf_op jit(solution)/shard_map/while/body/eval_jaxpr/all_to_all | solution.py:38
  148.0 10.5 %collective-permute-start = (bf16[256,512]{1,0:T(8,128)(2,1)S(1)}, bf16[256,512]{1,0:T(8,128)(2,1)}, u32[]{:S(2)}, u32[]{:S(2)}) collective-permute-start(bf16[256,512]{1,0:T(8,128)(2,1)S(1)} %get-tuple-element.1074), channel_id=1, source_target_pairs={{0,8},{8,16},{16,24},{1,9},{9,17},{17,25},{2,10},{10,18},{18,26},{... | collective-permute-start | bytes 786440 | tf_op jit(solution)/shard_map/while/body/eval_jaxpr/ppermute | solution.py:10
  163.5 9.9 %all-to-all-start = ((bf16[8,8,512]{2,1,0:T(8,128)(2,1)}), bf16[8,8,512]{2,1,0:T(8,128)(2,1)S(1)}, u32[]{:S(2)}, u32[]{:S(2)}) async-start(bf16[8,8,512]{2,1,0:T(8,128)(2,1)} %fusion.108), calls=%async_computation | async-start | bytes 131072 | tf_op jit(solution)/shard_map/while/body/eval_jaxpr/all_to_all | solution.py:38
  177.9 10.5 %collective-permute-start = (bf16[256,512]{1,0:T(8,128)(2,1)S(1)}, bf16[256,512]{1,0:T(8,128)(2,1)}, u32[]{:S(2)}, u32[]{:S(2)}) collective-permute-start(bf16[256,512]{1,0:T(8,128)(2,1)S(1)} %get-tuple-element.1074), channel_id=1, source_target_pairs={{0,8},{8,16},{16,24},{1,9},{9,17},{17,25},{2,10},{10,18},{18,26},{... | collective-permute-start | bytes 786440 | tf_op jit(solution)/shard_map/while/body/eval_jaxpr/ppermute | solution.py:10
  193.4 9.9 %all-to-all-start = ((bf16[8,8,512]{2,1,0:T(8,128)(2,1)}), bf16[8,8,512]{2,1,0:T(8,128)(2,1)S(1)}, u32[]{:S(2)}, u32[]{:S(2)}) async-start(bf16[8,8,512]{2,1,0:T(8,128)(2,1)} %fusion.108), calls=%async_computation | async-start | bytes 131072 | tf_op jit(solution)/shard_map/while/body/eval_jaxpr/all_to_all | solution.py:38
  207.8 10.5 %collective-permute-start = (bf16[256,512]{1,0:T(8,128)(2,1)S(1)}, bf16[256,512]{1,0:T(8,128)(2,1)}, u32[]{:S(2)}, u32[]{:S(2)}) collective-permute-start(bf16[256,512]{1,0:T(8,128)(2,1)S(1)} %get-tuple-element.1074), channel_id=1, source_target_pairs={{0,8},{8,16},{16,24},{1,9},{9,17},{17,25},{2,10},{10,18},{18,26},{... | collective-permute-start | bytes 786440 | tf_op jit(solution)/shard_map/while/body/eval_jaxpr/ppermute | solution.py:10
  229.6 9.7 %all-to-all-start.1 = ((bf16[8,8,512]{2,1,0:T(8,128)(2,1)}), bf16[8,8,512]{2,1,0:T(8,128)(2,1)S(1)}, u32[]{:S(2)}, u32[]{:S(2)}) async-start(bf16[8,8,512]{2,1,0:T(8,128)(2,1)} %slice_bitcast_fusion.2), calls=%async_computation.1 | async-start | bytes 131072 | tf_op jit(solution)/shard_map/while/body/eval_jaxpr/all_to_all | solution.py:98
  241.4 11.6 %collective-permute-start.1 = (bf16[256,512]{1,0:T(8,128)(2,1)S(1)}, bf16[256,512]{1,0:T(8,128)(2,1)S(1)}, u32[]{:S(2)}, u32[]{:S(2)}) collective-permute-start(bf16[256,512]{1,0:T(8,128)(2,1)S(1)} %get-tuple-element.1097), channel_id=1, source_target_pairs={{8,0},{16,8},{24,16},{9,1},{17,9},{25,17},{10,2},{18,10},{26,18},{... | collective-permute-start | bytes 786440 | tf_op jit(solution)/shard_map/while/body/eval_jaxpr/ppermute | solution.py:10
  259.3 9.4 %all-to-all-start.1 = ((bf16[8,8,512]{2,1,0:T(8,128)(2,1)}), bf16[8,8,512]{2,1,0:T(8,128)(2,1)S(1)}, u32[]{:S(2)}, u32[]{:S(2)}) async-start(bf16[8,8,512]{2,1,0:T(8,128)(2,1)} %slice_bitcast_fusion.2), calls=%async_computation.1 | async-start | bytes 131072 | tf_op jit(solution)/shard_map/while/body/eval_jaxpr/all_to_all | solution.py:98
  270.8 11.6 %collective-permute-start.1 = (bf16[256,512]{1,0:T(8,128)(2,1)S(1)}, bf16[256,512]{1,0:T(8,128)(2,1)S(1)}, u32[]{:S(2)}, u32[]{:S(2)}) collective-permute-start(bf16[256,512]{1,0:T(8,128)(2,1)S(1)} %get-tuple-element.1097), channel_id=1, source_target_pairs={{8,0},{16,8},{24,16},{9,1},{17,9},{25,17},{10,2},{18,10},{26,18},{... | collective-permute-start | bytes 786440 | tf_op jit(solution)/shard_map/while/body/eval_jaxpr/ppermute | solution.py:10
  288.7 9.4 %all-to-all-start.1 = ((bf16[8,8,512]{2,1,0:T(8,128)(2,1)}), bf16[8,8,512]{2,1,0:T(8,128)(2,1)S(1)}, u32[]{:S(2)}, u32[]{:S(2)}) async-start(bf16[8,8,512]{2,1,0:T(8,128)(2,1)} %slice_bitcast_fusion.2), calls=%async_computation.1 | async-start | bytes 131072 | tf_op jit(solution)/shard_map/while/body/eval_jaxpr/all_to_all | solution.py:98
  300.2 10.8 %collective-permute-start.1 = (bf16[256,512]{1,0:T(8,128)(2,1)S(1)}, bf16[256,512]{1,0:T(8,128)(2,1)S(1)}, u32[]{:S(2)}, u32[]{:S(2)}) collective-permute-start(bf16[256,512]{1,0:T(8,128)(2,1)S(1)} %get-tuple-element.1097), channel_id=1, source_target_pairs={{8,0},{16,8},{24,16},{9,1},{17,9},{25,17},{10,2},{18,10},{26,18},{... | collective-permute-start | bytes 786440 | tf_op jit(solution)/shard_map/while/body/eval_jaxpr/ppermute | solution.py:10
  328.8 10.8 %collective-permute-start.1 = (bf16[256,512]{1,0:T(8,128)(2,1)S(1)}, bf16[256,512]{1,0:T(8,128)(2,1)S(1)}, u32[]{:S(2)}, u32[]{:S(2)}) collective-permute-start(bf16[256,512]{1,0:T(8,128)(2,1)S(1)} %get-tuple-element.1097), channel_id=1, source_target_pairs={{8,0},{16,8},{24,16},{9,1},{17,9},{25,17},{10,2},{18,10},{26,18},{... | collective-permute-start | bytes 786440 | tf_op jit(solution)/shard_map/while/body/eval_jaxpr/ppermute | solution.py:10
  357.3 10.8 %collective-permute-start.1 = (bf16[256,512]{1,0:T(8,128)(2,1)S(1)}, bf16[256,512]{1,0:T(8,128)(2,1)S(1)}, u32[]{:S(2)}, u32[]{:S(2)}) collective-permute-start(bf16[256,512]{1,0:T(8,128)(2,1)S(1)} %get-tuple-element.1097), channel_id=1, source_target_pairs={{8,0},{16,8},{24,16},{9,1},{17,9},{25,17},{10,2},{18,10},{26,18},{... | collective-permute-start | bytes 786440 | tf_op jit(solution)/shard_map/while/body/eval_jaxpr/ppermute | solution.py:10
  385.9 10.8 %collective-permute-start.1 = (bf16[256,512]{1,0:T(8,128)(2,1)S(1)}, bf16[256,512]{1,0:T(8,128)(2,1)S(1)}, u32[]{:S(2)}, u32[]{:S(2)}) collective-permute-start(bf16[256,512]{1,0:T(8,128)(2,1)S(1)} %get-tuple-element.1097), channel_id=1, source_target_pairs={{8,0},{16,8},{24,16},{9,1},{17,9},{25,17},{10,2},{18,10},{26,18},{... | collective-permute-start | bytes 786440 | tf_op jit(solution)/shard_map/while/body/eval_jaxpr/ppermute | solution.py:10
  402.9 9.4 %all-to-all-start.1 = ((bf16[8,8,512]{2,1,0:T(8,128)(2,1)}), bf16[8,8,512]{2,1,0:T(8,128)(2,1)S(1)}, u32[]{:S(2)}, u32[]{:S(2)}) async-start(bf16[8,8,512]{2,1,0:T(8,128)(2,1)} %slice_bitcast_fusion.2), calls=%async_computation.1 | async-start | bytes 131072 | tf_op jit(solution)/shard_map/while/body/eval_jaxpr/all_to_all | solution.py:98
  414.4 10.8 %collective-permute-start.1 = (bf16[256,512]{1,0:T(8,128)(2,1)S(1)}, bf16[256,512]{1,0:T(8,128)(2,1)S(1)}, u32[]{:S(2)}, u32[]{:S(2)}) collective-permute-start(bf16[256,512]{1,0:T(8,128)(2,1)S(1)} %get-tuple-element.1097), channel_id=1, source_target_pairs={{8,0},{16,8},{24,16},{9,1},{17,9},{25,17},{10,2},{18,10},{26,18},{... | collective-permute-start | bytes 786440 | tf_op jit(solution)/shard_map/while/body/eval_jaxpr/ppermute | solution.py:10
  (38 other events, 408.9 us)
Sparse Core Ops, SparseCore 0:
  427.6 57.5 all-reduce.3
where the time goes:
time: 505 us; the launch traced here: 496 us
  starting transfers between devices  128 us (25%)
  waiting for transfers between devices  121 us (24%)
  matrix products  89.3 us (18%)
  local copies, waits for them, and re-layouts  74 us (15%)
  other arithmetic  69 us (14%)
  between operations  14.1 us (3%)
    ppermute x14, waiting for transfers between devices, from_behind(): lax.ppermute(value, axis, [(source, source + steps) for source in range(f...  63.1 us
    psum x1, waiting for transfers between devices, finish_grads(): lax.psum(grad_pair[0].astype(jnp.bfloat16), 'node').astype(jnp.float32)  57.7 us
    ppermute x14, starting transfers between devices, from_behind(): lax.ppermute(value, axis, [(source, source + steps) for source in range(f...  47.1 us
    all_to_all x7, starting transfers between devices, layer_forward(): lax.all_to_all(outgoing, 'node', split_axis=0, concat_axis=0, tiled=True)  41 us
    all_to_all x7, starting transfers between devices, layer_backward(): lax.all_to_all(remote, 'node', split_axis=0, concat_axis=0, tiled=True)  39.5 us
    dynamic_update_slice x28, other arithmetic, put_row(): lax.dynamic_update_index_in_dim(buffer, jnp.where(valid, value, current),...  36.2 us
    dynamic_slice x42, local copies, waits for them, and re-layouts, pick(): return lax.dynamic_index_in_dim(array, index, 0, keepdims=False)  32.9 us
    dot_general x7, matrix products, layer_backward(): lax.dot_general(aggregate, d_pre, over_rows, preferred_element_type=jnp.f...  17.9 us
  transfers between devices with their start and end apart: 29, of which 15 were waited for; matrix products, arithmetic and copies ran while one was open for 18% of the time, Pallas kernels for 0%

commit v1 on v0

v1 whole, which is shorter than its diff:
```python
import jax
import jax.numpy as jnp
from jax import lax
from jax.sharding import PartitionSpec as P


def pick(array, index):
    return lax.dynamic_index_in_dim(array, index, 0, keepdims=False)


def dot(a, b, dims=((1,), (0,))):
    return lax.dot_general(a, b, (dims, ((), ())), preferred_element_type=jnp.float32)


def dense_tiles(col_tiles, values, col_count):
    row_tiles, degree, tile, _ = values.shape
    chosen = col_tiles[:, :, None] == jnp.arange(col_count)[None, None, :]
    wide = jnp.where(chosen[:, :, :, None, None], values[:, :, None].astype(jnp.float32), 0.0)
    return jnp.sum(wide, axis=1).transpose(0, 2, 1, 3).reshape(row_tiles * tile, col_count * tile).astype(jnp.bfloat16)


def slot_selector(send_list, counts, node_rows):
    peers, slots = send_list.shape
    live = jnp.arange(slots)[None, :] < counts[:, None]
    hit = send_list[:, :, None] == jnp.arange(node_rows)[None, None, :]
    return (hit & live[:, :, None]).astype(jnp.bfloat16).reshape(peers * slots, node_rows)


def swap_rows(rows, peers):
    parts = rows.reshape(peers, -1, rows.shape[-1])
    return lax.all_to_all(parts, "node", split_axis=0, concat_axis=0, tiled=True).reshape(rows.shape)


def body(features, w_self, w_neigh, w_out, labels, train_mask, tile_cols, tile_vals, send_rows, send_counts):
    me = lax.axis_index("layer")
    layers = lax.axis_size("layer")
    peers = lax.axis_size("node")
    spans, node_rows, feat_dim = features.shape
    classes = w_out.shape[1]
    tile = tile_vals.shape[-1]
    slots = send_rows.shape[-1]
    received = peers * slots
    ext_rows = (node_rows + received + tile - 1) // tile * tile
    scale = 1.0 / (spans * node_rows * peers)
    bf16 = jnp.bfloat16

    adjacency = dense_tiles(pick(tile_cols, me)[0], pick(tile_vals, me)[0], ext_rows // tile)
    adjacency = adjacency[:, : node_rows + received]
    selector = slot_selector(pick(send_rows, me)[0], pick(send_counts, me)[0], node_rows)
    weights_self = lax.all_gather(w_self[0], "layer")
    weights_neigh = lax.all_gather(w_neigh[0], "layer")

    hidden = pick(features, me)
    saved = []
    acts = []
    for layer in range(layers):
        arrived = swap_rows(dot(selector, hidden).astype(bf16), peers)
        aggregate = dot(adjacency, jnp.concatenate([hidden, arrived], axis=0)).astype(bf16)
        preact = dot(hidden, weights_self[layer]) + dot(aggregate, weights_neigh[layer])
        saved.append((hidden, aggregate, preact))
        hidden = jax.nn.silu(preact).astype(bf16)
        acts.append(hidden)

    logits = dot(hidden, w_out)
    expo = jnp.exp(logits)
    probs = expo / jnp.sum(expo, axis=-1, keepdims=True)
    onehot = (pick(labels, me)[:, None] == jnp.arange(classes)[None, :]).astype(jnp.float32)
    g_logits = (pick(train_mask, me)[:, None].astype(jnp.float32) * (probs - onehot)).astype(bf16)
    d_out = dot(g_logits, w_out, ((1,), (1,))).astype(bf16)

    grads = [None] * layers
    weight_grads = [None] * layers
    for layer in range(layers - 1, -1, -1):
        hidden_in, aggregate, preact = saved[layer]
        sigma = jax.nn.sigmoid(preact)
        d_pre = (d_out.astype(jnp.float32) * (sigma * (1.0 + preact * (1.0 - sigma)))).astype(bf16)
        d_agg = dot(d_pre, weights_neigh[layer], ((1,), (1,))).astype(bf16)
        d_ext = dot(adjacency, d_agg, ((0,), (0,)))
        returned = swap_rows(d_ext[node_rows:].astype(bf16), peers)
        weight_grads[layer] = jnp.stack(
            [dot(hidden_in, d_pre, ((0,), (0,))), dot(aggregate, d_pre, ((0,), (0,)))]
        ).astype(bf16)
        back_self = dot(d_pre, weights_self[layer], ((1,), (1,)))
        scattered = dot(selector, returned, ((0,), (0,)))
        d_out = (back_self + d_ext[:node_rows] + scattered).astype(bf16)
        grads[layer] = d_out

    layer_acts = lax.all_to_all(jnp.stack(acts), "layer", split_axis=0, concat_axis=0, tiled=True)
    act_grads = lax.all_to_all(jnp.stack(grads), "layer", split_axis=0, concat_axis=0, tiled=True)
    mine = lax.all_to_all(jnp.stack(weight_grads), "layer", split_axis=0, concat_axis=0, tiled=True)
    mine = jnp.sum(mine.astype(jnp.float32), axis=0).astype(bf16)
    total = lax.psum(mine, "node").astype(jnp.float32) * scale
    return layer_acts[None], act_grads[None], total[0][None], total[1][None]


def solution(mesh):
    in_specs = (
        P(None, "node", None),
        P("layer", None, None),
        P("layer", None, None),
        P(),
        P(None, "node"),
        P(None, "node"),
        P(None, "node", None, None),
        P(None, "node", None, None, None, None),
        P(None, "node", None, None),
        P(None, "node", None),
    )
    out_specs = (
        P("layer", None, "node", None),
        P("layer", None, "node", None),
        P("layer", None, None),
        P("layer", None, None),
    )
    return jax.shard_map(body, mesh=mesh, in_specs=in_specs, out_specs=out_specs, check_vma=False)
```

time: 505 us -> 332 us (0.66)
  starting transfers between devices: 128 us -> 62.8 us
  local copies, waits for them, and re-layouts: 74 us -> 9.73 us
  waiting for transfers between devices: 121 us -> 184 us
  other arithmetic: 69 us -> 13.6 us
  matrix products: 89.3 us -> 42.2 us
    all_to_all x14 -> x11, waiting for transfers between devices: 0.04 us -> 71.3 us  [the longest x1 44 us: body(): lax.all_to_all(jnp.stack(weight_grads), 'layer', split_axis=0, concat_axi...]
    ppermute x14 -> x0, waiting for transfers between devices: 63.1 us -> none  [from_behind(): lax.ppermute(value, axis, [(source, source + steps) for source in range(f...]
    all_gather x0 -> x2, waiting for transfers between devices: none -> 61.5 us  [the longest x1 35.8 us: body(): weights_neigh = lax.all_gather(w_neigh[0], 'layer')]
    dot_general x65 -> x38, matrix products: 89.3 us -> 42.2 us  [dot(): lax.dot_general(a, b, (dims, ((), ())), preferred_element_type=jnp.float32)]
    ppermute x14 -> x0, starting transfers between devices: 47.1 us -> none  [from_behind(): lax.ppermute(value, axis, [(source, source + steps) for source in range(f...]
    dynamic_update_slice x28 -> x0, other arithmetic: 36.2 us -> none  [put_row(): lax.dynamic_update_index_in_dim(buffer, jnp.where(valid, value, current),...]
    dynamic_slice x42 -> x1, local copies, waits for them, and re-layouts: 32.9 us -> 0.69 us  [pick(): return lax.dynamic_index_in_dim(array, index, 0, keepdims=False)]
    all_to_all x14 -> x11, starting transfers between devices: 80.5 us -> 62.6 us  [the longest x8 50.7 us: swap_rows(): lax.all_to_all(parts, 'node', split_axis=0, concat_axis=0, tiled=True)]
  transfers between devices with their start and end apart: 29 -> 14, of which waited for: 15 -> 13; matrix products, arithmetic and copies ran while one was open for 18% -> 8% of each run, Pallas kernels for 0% -> 0%
where the time goes in v1:
time: 332 us; the launch traced here: 326 us
  waiting for transfers between devices  184 us (55%)
  starting transfers between devices  62.8 us (19%)
  matrix products  42.2 us (13%)
  between operations  14.1 us (4%)
  other arithmetic  13.6 us (4%)
  local copies, waits for them, and re-layouts  9.73 us (3%)
    all_to_all x8, starting transfers between devices, swap_rows(): lax.all_to_all(parts, 'node', split_axis=0, concat_axis=0, tiled=True)  50.7 us
    psum x1, waiting for transfers between devices, body(): total = lax.psum(mine, 'node').astype(jnp.float32) * scale  49.5 us
    all_to_all x1, waiting for transfers between devices, body(): lax.all_to_all(jnp.stack(weight_grads), 'layer', split_axis=0, concat_axi...  44 us
    dot_general x38, matrix products, dot(): lax.dot_general(a, b, (dims, ((), ())), preferred_element_type=jnp.float32)  42.2 us
    all_gather x1, waiting for transfers between devices, body(): weights_neigh = lax.all_gather(w_neigh[0], 'layer')  35.8 us
    all_gather x1, waiting for transfers between devices, body(): weights_self = lax.all_gather(w_self[0], 'layer')  25.7 us
    all_to_all x8, waiting for transfers between devices, swap_rows(): lax.all_to_all(parts, 'node', split_axis=0, concat_axis=0, tiled=True)  9.4 us
    all_to_all x1, waiting for transfers between devices, body(): lax.all_to_all(jnp.stack(acts), 'layer', split_axis=0, concat_axis=0, til...  9.09 us
  transfers between devices with their start and end apart: 14, of which 13 were waited for; matrix products, arithmetic and copies ran while one was open for 8% of the time, Pallas kernels for 0%

profile of v1, /device:TPU:25, one launch (start us, length us, event | category | flops | bytes accessed | tf_op | source)
XLA Modules:
  0.0 326.1 jit_solution(3191067268487426400)
XLA Ops:
  11.1 5.4 %all-to-all-start = ((bf16[8,8,512]{2,1,0:T(8,128)(2,1)}), bf16[8,8,512]{2,1,0:T(8,128)(2,1)S(1)}, u32[]{:S(2)}, u32[]{:S(2)}) async-start(bf16[8,8,512]{2,1,0:T(8,128)(2,1)} %fusion.24), calls=%async_computation | async-start | bytes 131072 | tf_op jit(solution)/shard_map/all_to_all | solution.py:31
  20.5 25.7 %all-gather.3.cloned.1.call-done = bf16[4,512,512]{2,1,0:T(8,128)(2,1)} async-done(((bf16[1,512,512]{2,1,0:T(8,128)(2,1)}), bf16[4,512,512]{2,1,0:T(8,128)(2,1)}) %all-gather.3.cloned.1.call-update) | async-done | bytes 2097168 | tf_op jit(solution)/shard_map/all_gather | solution.py:50
  47.5 35.8 %all-gather.5.cloned.1.call-done = bf16[4,512,512]{2,1,0:T(8,128)(2,1)} async-done(((bf16[1,512,512]{2,1,0:T(8,128)(2,1)}), bf16[4,512,512]{2,1,0:T(8,128)(2,1)}) %all-gather.5.cloned.1.call-update) | async-done | bytes 2097168 | tf_op jit(solution)/shard_map/all_gather | solution.py:51
  83.4 2.1 multiply_convert_fusion.6
  86.4 5.4 %all-to-all-start.1 = ((bf16[8,8,512]{2,1,0:T(8,128)(2,1)}), bf16[8,8,512]{2,1,0:T(8,128)(2,1)S(1)}, u32[]{:S(2)}, u32[]{:S(2)}) async-start(bf16[8,8,512]{2,1,0:T(8,128)(2,1)} %fusion.25), calls=%async_computation.1 | async-start | bytes 131072 | tf_op jit(solution)/shard_map/all_to_all | solution.py:31
  94.7 2.2 multiply_convert_fusion.5
  97.8 6.6 %all-to-all-start.2 = ((bf16[8,8,512]{2,1,0:T(8,128)(2,1)}), bf16[8,8,512]{2,1,0:T(8,128)(2,1)S(1)}, u32[]{:S(2)}, u32[]{:S(2)}) async-start(bf16[8,8,512]{2,1,0:T(8,128)(2,1)} %fusion.26), calls=%async_computation.2 | async-start | bytes 131072 | tf_op jit(solution)/shard_map/all_to_all | solution.py:31
  107.3 2.2 multiply_convert_fusion.4
  110.4 6.7 %all-to-all-start.3 = ((bf16[8,8,512]{2,1,0:T(8,128)(2,1)}), bf16[8,8,512]{2,1,0:T(8,128)(2,1)S(1)}, u32[]{:S(2)}, u32[]{:S(2)}) async-start(bf16[8,8,512]{2,1,0:T(8,128)(2,1)} %fusion.27), calls=%async_computation.3 | async-start | bytes 131072 | tf_op jit(solution)/shard_map/all_to_all | solution.py:31
  126.4 6.7 %all-to-all-start.5 = ((bf16[8,8,512]{2,1,0:T(8,128)(2,1)}), bf16[8,8,512]{2,1,0:T(8,128)(2,1)S(1)}, u32[]{:S(2)}, u32[]{:S(2)}) async-start(bf16[8,8,512]{2,1,0:T(8,128)(2,1)} %fusion.47), calls=%async_computation.5 | async-start | bytes 131072 | tf_op jit(solution)/shard_map/all_to_all | solution.py:31
  136.0 2.4 multiply_convert_fusion.2
  141.7 6.7 %all-to-all-start.6 = ((bf16[8,8,512]{2,1,0:T(8,128)(2,1)}), bf16[8,8,512]{2,1,0:T(8,128)(2,1)S(1)}, u32[]{:S(2)}, u32[]{:S(2)}) async-start(bf16[8,8,512]{2,1,0:T(8,128)(2,1)} %fusion.48), calls=%async_computation.6 | async-start | bytes 131072 | tf_op jit(solution)/shard_map/all_to_all | solution.py:31
  156.3 6.7 %all-to-all-start.7 = ((bf16[8,8,512]{2,1,0:T(8,128)(2,1)}), bf16[8,8,512]{2,1,0:T(8,128)(2,1)S(1)}, u32[]{:S(2)}, u32[]{:S(2)}) async-start(bf16[8,8,512]{2,1,0:T(8,128)(2,1)} %fusion.49), calls=%async_computation.7 | async-start | bytes 131072 | tf_op jit(solution)/shard_map/all_to_all | solution.py:31
  165.8 2.3 multiply_convert_fusion
  170.4 6.6 %all-to-all-start.8 = ((bf16[8,8,512]{2,1,0:T(8,128)(2,1)}), bf16[8,8,512]{2,1,0:T(8,128)(2,1)S(1)}, u32[]{:S(2)}, u32[]{:S(2)}) async-start(bf16[8,8,512]{2,1,0:T(8,128)(2,1)} %fusion.50), calls=%async_computation.8 | async-start | bytes 131072 | tf_op jit(solution)/shard_map/all_to_all | solution.py:31
  180.2 3.5 %all-to-all-start.4 = ((bf16[4,256,512]{2,1,0:T(8,128)(2,1)}), bf16[4,256,512]{2,1,0:T(8,128)(2,1)S(1)}, u32[]{:S(2)}, u32[]{:S(2)}) async-start(bf16[4,256,512]{2,1,0:T(8,128)(2,1)} %pad_maximum_fusion), calls=%async_computation.4 | async-start | bytes 2097152 | tf_op jit(solution)/shard_map/all_to_all | solution.py:88
  184.0 3.7 %maximum_maximum_fusion = bf16[4,2,512,512]{3,2,1,0:T(8,128)(2,1)} fusion(bf16[1,1,512,512]{3,2,1,0:T(8,128)(2,1)} %fusion.7, bf16[1,1,512,512]{3,2,1,0:T(8,128)(2,1)} %fusion.6, bf16[1,1,512,512]{3,2,1,0:T(8,128)(2,1)} %fusion.5, bf16[1,1,512,512]{3,2,1,0:T(8,128)(2,1)} %fusion.4, bf16[1,1,512,512]{3,2,1,0:T(8,128)(2,1)} %fusion.3, ...), kind=kLoop, calls=%fused_computation | loop fusion | flops 14680064 | bytes 8388608 | tf_op jit(solution)/shard_map/stack | solution.py:90
  187.7 9.1 %all-to-all-done.4 = bf16[4,256,512]{2,1,0:T(8,128)(2,1)S(1)} async-done(((bf16[4,256,512]{2,1,0:T(8,128)(2,1)}), bf16[4,256,512]{2,1,0:T(8,128)(2,1)S(1)}, u32[]{:S(2)}, u32[]{:S(2)}) %all-to-all-start.4) | async-done | bytes 1048608 | tf_op jit(solution)/shard_map/all_to_all | solution.py:88
  196.8 4.9 %all-to-all-start.10 = ((bf16[4,2,512,512]{3,2,1,0:T(8,128)(2,1)}), bf16[4,2,512,512]{3,2,1,0:T(8,128)(2,1)}, u32[]{:S(2)}, u32[]{:S(2)}) async-start(bf16[4,2,512,512]{3,2,1,0:T(8,128)(2,1)} %maximum_maximum_fusion), calls=%async_computation.10 | async-start | bytes 8388608 | tf_op jit(solution)/shard_map/all_to_all | solution.py:90
  204.6 44.0 %all-to-all-done.10 = bf16[4,2,512,512]{3,2,1,0:T(8,128)(2,1)} async-done(((bf16[4,2,512,512]{3,2,1,0:T(8,128)(2,1)}), bf16[4,2,512,512]{3,2,1,0:T(8,128)(2,1)}, u32[]{:S(2)}, u32[]{:S(2)}) %all-to-all-start.10) | async-done | bytes 4194336 | tf_op jit(solution)/shard_map/all_to_all | solution.py:90
  248.5 3.5 %all-to-all-start.9 = ((bf16[4,256,512]{2,1,0:T(8,128)(2,1)}), bf16[4,256,512]{2,1,0:T(8,128)(2,1)S(1)}, u32[]{:S(2)}, u32[]{:S(2)}) async-start(bf16[4,256,512]{2,1,0:T(8,128)(2,1)} %pad_maximum_fusion.1), calls=%async_computation.9 | async-start | bytes 2097152 | tf_op jit(solution)/shard_map/all_to_all | solution.py:89
  252.1 4.1 %reduce_sum.32 = bf16[2,512,512]{2,1,0:T(8,128)(2,1)} reduce(bf16[4,2,512,512]{3,2,1,0:T(8,128)(2,1)} %all-to-all-done.10, bf16[]{:T(256)} %constant.44.clone.1), dimensions={0}, to_apply=%region_2.3 | reduce | flops 1572864 | bytes 5242882 | tf_op jit(solution)/shard_map/reduce_sum | solution.py:91
  256.3 8.9 %all-to-all-done.9 = bf16[4,256,512]{2,1,0:T(8,128)(2,1)S(1)} async-done(((bf16[4,256,512]{2,1,0:T(8,128)(2,1)}), bf16[4,256,512]{2,1,0:T(8,128)(2,1)S(1)}, u32[]{:S(2)}, u32[]{:S(2)}) %all-to-all-start.9) | async-done | bytes 1048608 | tf_op jit(solution)/shard_map/all_to_all | solution.py:89
  265.1 49.5 %all-reduce.2.cloned.1.call-done = bf16[2,512,512]{2,1,0:T(8,128)(2,1)} async-done(((bf16[2,512,512]{2,1,0:T(8,128)(2,1)}), bf16[2,512,512]{2,1,0:T(8,128)(2,1)}) %all-reduce.2.cloned.1.call-update) | async-done | bytes 1048592 | tf_op jit(solution)/shard_map/psum | solution.py:92
  (95 shorter events, 57.3 us)
Async XLA Ops:
  7.2 3.1 copy-start
  7.2 39.0 %all-gather.3.cloned.1.call-start = ((), (), s32[]{:S(2)}) async-start(), calls=%async_computation.11 | async-start | bytes 2621440 | tf_op jit(solution)/shard_map/all_gather | solution.py:50
  7.9 75.5 %all-gather.5.cloned.1.call-start = ((), (), s32[]{:S(2)}) async-start(), calls=%async_computation.12 | async-start | bytes 2621440 | tf_op jit(solution)/shard_map/all_gather | solution.py:51
  11.1 9.0 %all-to-all-start = ((bf16[8,8,512]{2,1,0:T(8,128)(2,1)}), bf16[8,8,512]{2,1,0:T(8,128)(2,1)S(1)}, u32[]{:S(2)}, u32[]{:S(2)}) async-start(bf16[8,8,512]{2,1,0:T(8,128)(2,1)} %fusion.24), calls=%async_computation | async-start | bytes 131072 | tf_op jit(solution)/shard_map/all_to_all | solution.py:31
  20.5 65.0 %copy-start.1 = (bf16[256,512]{1,0:T(8,128)(2,1)}, bf16[256,512]{1,0:T(8,128)(2,1)S(1)}, u32[]{:S(2)}) copy-start(bf16[256,512]{1,0:T(8,128)(2,1)S(1)} %convolution_convert_fusion.16) | copy-start | bytes 786436
  86.4 8.0 %all-to-all-start.1 = ((bf16[8,8,512]{2,1,0:T(8,128)(2,1)}), bf16[8,8,512]{2,1,0:T(8,128)(2,1)S(1)}, u32[]{:S(2)}, u32[]{:S(2)}) async-start(bf16[8,8,512]{2,1,0:T(8,128)(2,1)} %fusion.25), calls=%async_computation.1 | async-start | bytes 131072 | tf_op jit(solution)/shard_map/all_to_all | solution.py:31
  94.7 2.3 copy-start.3
  97.8 9.2 %all-to-all-start.2 = ((bf16[8,8,512]{2,1,0:T(8,128)(2,1)}), bf16[8,8,512]{2,1,0:T(8,128)(2,1)S(1)}, u32[]{:S(2)}, u32[]{:S(2)}) async-start(bf16[8,8,512]{2,1,0:T(8,128)(2,1)} %fusion.26), calls=%async_computation.2 | async-start | bytes 131072 | tf_op jit(solution)/shard_map/all_to_all | solution.py:31
  107.3 2.3 copy-start.5
  110.4 9.2 %all-to-all-start.3 = ((bf16[8,8,512]{2,1,0:T(8,128)(2,1)}), bf16[8,8,512]{2,1,0:T(8,128)(2,1)S(1)}, u32[]{:S(2)}, u32[]{:S(2)}) async-start(bf16[8,8,512]{2,1,0:T(8,128)(2,1)} %fusion.27), calls=%async_computation.3 | async-start | bytes 131072 | tf_op jit(solution)/shard_map/all_to_all | solution.py:31
  119.6 1.8 copy-start.9
  126.4 9.2 %all-to-all-start.5 = ((bf16[8,8,512]{2,1,0:T(8,128)(2,1)}), bf16[8,8,512]{2,1,0:T(8,128)(2,1)S(1)}, u32[]{:S(2)}, u32[]{:S(2)}) async-start(bf16[8,8,512]{2,1,0:T(8,128)(2,1)} %fusion.47), calls=%async_computation.5 | async-start | bytes 131072 | tf_op jit(solution)/shard_map/all_to_all | solution.py:31
  136.0 2.4 copy-start.6
  141.7 9.2 %all-to-all-start.6 = ((bf16[8,8,512]{2,1,0:T(8,128)(2,1)}), bf16[8,8,512]{2,1,0:T(8,128)(2,1)S(1)}, u32[]{:S(2)}, u32[]{:S(2)}) async-start(bf16[8,8,512]{2,1,0:T(8,128)(2,1)} %fusion.48), calls=%async_computation.6 | async-start | bytes 131072 | tf_op jit(solution)/shard_map/all_to_all | solution.py:31
  156.3 9.2 %all-to-all-start.7 = ((bf16[8,8,512]{2,1,0:T(8,128)(2,1)}), bf16[8,8,512]{2,1,0:T(8,128)(2,1)S(1)}, u32[]{:S(2)}, u32[]{:S(2)}) async-start(bf16[8,8,512]{2,1,0:T(8,128)(2,1)} %fusion.49), calls=%async_computation.7 | async-start | bytes 131072 | tf_op jit(solution)/shard_map/all_to_all | solution.py:31
  165.8 11.2 %copy-start.2 = (bf16[256,512]{1,0:T(8,128)(2,1)S(1)}, bf16[256,512]{1,0:T(8,128)(2,1)}, u32[]{:S(2)}) copy-start(bf16[256,512]{1,0:T(8,128)(2,1)} %copy-done.1) | copy-start | bytes 786436
  170.4 9.2 %all-to-all-start.8 = ((bf16[8,8,512]{2,1,0:T(8,128)(2,1)}), bf16[8,8,512]{2,1,0:T(8,128)(2,1)S(1)}, u32[]{:S(2)}, u32[]{:S(2)}) async-start(bf16[8,8,512]{2,1,0:T(8,128)(2,1)} %fusion.50), calls=%async_computation.8 | async-start | bytes 131072 | tf_op jit(solution)/shard_map/all_to_all | solution.py:31
  180.2 16.6 %all-to-all-start.4 = ((bf16[4,256,512]{2,1,0:T(8,128)(2,1)}), bf16[4,256,512]{2,1,0:T(8,128)(2,1)S(1)}, u32[]{:S(2)}, u32[]{:S(2)}) async-start(bf16[4,256,512]{2,1,0:T(8,128)(2,1)} %pad_maximum_fusion), calls=%async_computation.4 | async-start | bytes 2097152 | tf_op jit(solution)/shard_map/all_to_all | solution.py:88
  187.7 14.0 %copy-start.11 = (bf16[8,8,512]{2,1,0:T(8,128)(2,1)S(1)}, bf16[8,8,512]{2,1,0:T(8,128)(2,1)}, u32[]{:S(2)}) copy-start(bf16[8,8,512]{2,1,0:T(8,128)(2,1)} %copy-done.10) | copy-start | bytes 196612
  196.8 51.7 %all-to-all-start.10 = ((bf16[4,2,512,512]{3,2,1,0:T(8,128)(2,1)}), bf16[4,2,512,512]{3,2,1,0:T(8,128)(2,1)}, u32[]{:S(2)}, u32[]{:S(2)}) async-start(bf16[4,2,512,512]{3,2,1,0:T(8,128)(2,1)} %maximum_maximum_fusion), calls=%async_computation.10 | async-start | bytes 8388608 | tf_op jit(solution)/shard_map/all_to_all | solution.py:90
  201.7 1.7 copy-start.7
  201.7 1.7 copy-start.8
  248.5 16.6 %all-to-all-start.9 = ((bf16[4,256,512]{2,1,0:T(8,128)(2,1)}), bf16[4,256,512]{2,1,0:T(8,128)(2,1)S(1)}, u32[]{:S(2)}, u32[]{:S(2)}) async-start(bf16[4,256,512]{2,1,0:T(8,128)(2,1)} %pad_maximum_fusion.1), calls=%async_computation.9 | async-start | bytes 2097152 | tf_op jit(solution)/shard_map/all_to_all | solution.py:89
  252.1 62.5 %all-reduce.2.cloned.1.call-start = ((), (), s32[]{:S(2)}) async-start(), calls=%async_computation.13 | async-start | bytes 2097152 | tf_op jit(solution)/shard_map/psum | solution.py:92
  (2 other events, 2.3 us)
Sparse Core Ops, SparseCore 0:
  9.9 36.2 all-gather.2
  48.0 35.2 all-gather.4
  256.4 58.1 all-reduce.1

commit v2 on v1

v2 whole, which is shorter than its diff:
```python
import functools

import jax
import jax.numpy as jnp
from jax import lax
from jax.experimental import pallas as pl
from jax.experimental.pallas import tpu as pltpu
from jax.sharding import PartitionSpec as P


def pick(array, index):
    return lax.dynamic_index_in_dim(array, index, 0, keepdims=False)


def dot(a, b, dims=((1,), (0,))):
    return lax.dot_general(a, b, (dims, ((), ())), preferred_element_type=jnp.float32)


def dense_tiles(col_tiles, values, col_count):
    row_tiles, degree, tile, _ = values.shape
    chosen = col_tiles[:, :, None] == jnp.arange(col_count)[None, None, :]
    wide = jnp.where(chosen[:, :, :, None, None], values[:, :, None].astype(jnp.float32), 0.0)
    return jnp.sum(wide, axis=1).transpose(0, 2, 1, 3).reshape(row_tiles * tile, col_count * tile).astype(jnp.bfloat16)


def slot_selector(send_list, counts, node_rows):
    peers, slots = send_list.shape
    live = jnp.arange(slots)[None, :] < counts[:, None]
    hit = send_list[:, :, None] == jnp.arange(node_rows)[None, None, :]
    return (hit & live[:, :, None]).astype(jnp.bfloat16).reshape(peers * slots, node_rows)


MESH = pl.DeviceIdType.MESH


def window_kernel(
    layers, peers, slots, classes, scale,
    feats, w_self, w_neigh, w_out, labels, mask, adj, adj_t, sel, sel_t,
    acts_out, grads_out, gself_out, gneigh_out,
    hid, agg, pre, dpre, dout, wts, ext, back, outbox, inbox, rec_hid, rec_agg, rec_dpre,
    gsum, gsend, gsib, chip, parts, final,
    w_send, w_recv, f_send, f_recv, x_send, x_recv, blk_send, blk_recv,
    sib_send, sib_recv, rs_send, rs_recv, ag_send, ag_recv, fw_send, fw_recv,
):
    me = lax.axis_index("layer")
    node = lax.axis_index("node")
    core = lax.rem(node, 2)
    chip_at = node // 2
    chips = peers // 2
    sibling = node + 1 - 2 * core
    node_rows, feat_dim = hid.shape[1:]
    f32, bf16 = jnp.float32, jnp.bfloat16
    chunk = feat_dim // chips

    def remote(src, dst, send, recv, device):
        return pltpu.make_async_remote_copy(
            src_ref=src, dst_ref=dst, send_sem=send, recv_sem=recv, device_id=device, device_id_type=MESH
        )

    def drain(ref, sem):
        pltpu.make_async_copy(ref, ref, sem).wait()

    def each(count, fn, start=0):
        def step(i, carry):
            fn(i)
            return carry
        lax.fori_loop(start, count, step, 0)

    def other_layers(fn):
        each(layers, lambda i: fn(lax.rem(me + i, layers)), 1)

    def other_nodes(fn):
        each(peers, lambda i: fn(lax.rem(node + i, peers)), 1)

    def other_chips(fn):
        each(chips, lambda i: fn(lax.rem(chip_at + i, chips)), 1)

    barrier = pltpu.get_barrier_semaphore()
    other_layers(lambda i: pl.semaphore_signal(barrier, inc=1, device_id=(i, node), device_id_type=MESH))
    other_nodes(lambda i: pl.semaphore_signal(barrier, inc=1, device_id=(me, i), device_id_type=MESH))
    wts[me, 0] = w_self[...]
    wts[me, 1] = w_neigh[...]
    pl.semaphore_wait(barrier, layers - 1 + peers - 1)

    def send_weights(i):
        remote(wts.at[me, core], wts.at[me, core], w_send.at[i], w_recv.at[me], (i, node)).start()

    other_layers(send_weights)

    hid[0] = feats[me]
    ext[...] = jnp.zeros_like(ext)
    back[...] = jnp.zeros_like(back)

    @pl.when(me == 0)
    def _():
        rec_hid[...] = feats[...]

    def swap_start(turn):
        def send(i):
            remote(
                outbox.at[turn, pl.ds(pl.multiple_of(i * slots, slots), slots)],
                inbox.at[turn, pl.ds(pl.multiple_of(node * slots, slots), slots)],
                x_send.at[turn], x_recv.at[turn], (me, i),
            ).start()
        other_nodes(send)
        mine = pl.ds(pl.multiple_of(node * slots, slots), slots)
        inbox[turn, mine] = outbox[turn, mine]

    def swap_bytes(turn):
        return inbox.at[turn, pl.ds(0, (peers - 1) * slots)]

    def give(kind, src, dst, owner):
        @pl.when(owner == me)
        def _():
            dst[me] = src[...]

        @pl.when(owner != me)
        def _():
            remote(src, dst.at[me], blk_send.at[kind, owner], blk_recv.at[kind, me], (owner, node)).start()

    def forward(layer):
        outbox[layer] = dot(sel[...], hid[layer])
        swap_start(layer)

        @pl.when(layer != me)
        def _():
            drain(wts.at[layer, core], w_recv.at[layer])
            remote(wts.at[layer, core], wts.at[layer, core], f_send.at[layer], f_recv.at[layer], (me, sibling)).start()

        ext[:node_rows] = hid[layer]
        drain(swap_bytes(layer), x_recv.at[layer])
        ext[node_rows : node_rows + peers * slots] = inbox[layer, : peers * slots].astype(bf16)
        aggregate = dot(adj[...], ext[...]).astype(bf16)
        agg[layer] = aggregate
        give(0, agg.at[layer], rec_agg, layer)

        @pl.when(layer != me)
        def _():
            drain(wts.at[layer, 1 - core], f_recv.at[layer])

        preact = dot(hid[layer], wts[layer, 0]) + dot(aggregate, wts[layer, 1])
        pre[layer] = preact
        hid[layer + 1] = (preact * jax.nn.sigmoid(preact)).astype(bf16)
        give(1, hid.at[layer + 1], acts_out, layer)

        @pl.when(layer + 1 < layers)
        def _():
            give(2, hid.at[layer + 1], rec_hid, lax.rem(layer + 1, layers))

    each(layers, forward)

    logits = dot(hid[layers], w_out[...])
    real = lax.broadcasted_iota(jnp.int32, logits.shape, 1)
    expo = jnp.where(real < classes, jnp.exp(logits), 0.0)
    probs = expo / jnp.sum(expo, axis=-1, keepdims=True)
    onehot = (labels[...] == real).astype(f32)
    g_logits = (mask[...].astype(f32) * (probs - onehot)).astype(bf16)
    dout[layers] = dot(g_logits, w_out[...], ((1,), (1,))).astype(bf16)

    def backward(turn):
        layer = layers - 1 - turn
        preact = pre[layer]
        sigma = jax.nn.sigmoid(preact)
        d_pre = (dout[layer + 1].astype(f32) * (sigma * (1.0 + preact * (1.0 - sigma)))).astype(bf16)
        dpre[layer] = d_pre
        d_agg = dot(d_pre, wts[layer, 1], ((1,), (1,))).astype(bf16)
        d_ext = dot(adj_t[...], d_agg)
        outbox[layers + turn] = d_ext[node_rows:]
        swap_start(layers + turn)
        give(3, dpre.at[layer], rec_dpre, layer)
        local = dot(d_pre, wts[layer, 0], ((1,), (1,))) + d_ext[:node_rows]
        drain(swap_bytes(layers + turn), x_recv.at[layers + turn])
        back[: peers * slots] = inbox[layers + turn, : peers * slots].astype(bf16)
        dout[layer] = (local + dot(sel_t[...], back[...])).astype(bf16)
        give(4, dout.at[layer], grads_out, layer)

    each(layers, backward)

    gsum[...] = jnp.zeros_like(gsum)

    def add_span(i):
        span = lax.rem(me + i, layers)

        @pl.when(i != 0)
        def _():
            drain(rec_agg.at[span], blk_recv.at[0, span])
            drain(rec_dpre.at[span], blk_recv.at[3, span])

            @pl.when(me != 0)
            def _():
                drain(rec_hid.at[span], blk_recv.at[2, span])

        over_rows = ((0,), (0,))
        gsum[0] += dot(rec_hid[span], rec_dpre[span], over_rows)
        gsum[1] += dot(rec_agg[span], rec_dpre[span], over_rows)

    each(layers, add_span)

    gsend[...] = gsum[1 - core].astype(bf16)
    to_sibling = remote(gsend, gsib, sib_send, sib_recv, (me, sibling))
    to_sibling.start()
    drain(gsib, sib_recv)
    chip[...] = (gsum[core] + gsib[...].astype(f32)).astype(bf16)

    def rows_of(i):
        return pl.ds(pl.multiple_of(i * chunk, chunk), chunk)

    def send_part(i):
        remote(chip.at[rows_of(i)], parts.at[rows_of(chip_at)], rs_send, rs_recv, (me, 2 * i + core)).start()

    other_chips(send_part)
    parts[rows_of(chip_at)] = chip[rows_of(chip_at)]
    drain(parts.at[pl.ds(0, (chips - 1) * chunk)], rs_recv)
    total = parts[pl.ds(0, chunk)].astype(f32)
    for i in range(1, chips):
        total = total + parts[pl.ds(i * chunk, chunk)].astype(f32)
    final[core, rows_of(chip_at)] = total.astype(bf16)

    def send_final(i):
        mine = final.at[core, rows_of(chip_at)]
        remote(mine, mine, ag_send, ag_recv.at[chip_at], (me, 2 * i + core)).start()

    def pass_on(i):
        piece = final.at[core, rows_of(i)]
        remote(piece, piece, fw_send, fw_recv.at[i], (me, sibling)).start()

    other_chips(send_final)
    pass_on(chip_at)

    def take_final(i):
        drain(final.at[core, rows_of(i)], ag_recv.at[i])
        pass_on(i)

    other_chips(take_final)
    each(chips, lambda i: drain(final.at[1 - core, rows_of(i)], fw_recv.at[i]))
    gself_out[...] = final[0].astype(f32) * scale
    gneigh_out[...] = final[1].astype(f32) * scale

    def finish_layer(i):
        drain(acts_out.at[i], blk_recv.at[1, i])
        drain(grads_out.at[i], blk_recv.at[4, i])
        drain(wts.at[me, core], w_send.at[i])
        drain(wts.at[i, core], f_send.at[i])
        drain(agg.at[i], blk_send.at[0, i])
        drain(hid.at[i], blk_send.at[1, i])
        drain(dpre.at[i], blk_send.at[3, i])
        drain(dout.at[i], blk_send.at[4, i])

        @pl.when(i != 0)
        def _():
            drain(hid.at[i], blk_send.at[2, i])

    other_layers(finish_layer)
    each(2 * layers, lambda turn: drain(swap_bytes(turn), x_send.at[turn]))
    drain(gsend, sib_send)
    drain(parts.at[pl.ds(0, (chips - 1) * chunk)], rs_send)
    drain(final.at[0, pl.ds(0, (chips - 1) * chunk)], ag_send)
    drain(final.at[0], fw_send)


def body(features, w_self, w_neigh, w_out, labels, train_mask, tile_cols, tile_vals, send_rows, send_counts):
    me = lax.axis_index("layer")
    layers = lax.axis_size("layer")
    peers = lax.axis_size("node")
    spans, node_rows, feat_dim = features.shape
    classes = w_out.shape[1]
    tile = tile_vals.shape[-1]
    slots = send_rows.shape[-1]
    ext_rows = (node_rows + peers * slots + tile - 1) // tile * tile
    slot_rows = ext_rows - node_rows
    chips = peers // 2
    chunk = feat_dim // chips
    scale = 1.0 / (spans * node_rows * peers)
    f32, bf16 = jnp.float32, jnp.bfloat16

    adjacency = dense_tiles(pick(tile_cols, me)[0], pick(tile_vals, me)[0], ext_rows // tile)
    selector = slot_selector(pick(send_rows, me)[0], pick(send_counts, me)[0], node_rows)
    selector = jnp.pad(selector, ((0, slot_rows - peers * slots), (0, 0)))
    w_out = jnp.pad(w_out, ((0, 0), (0, -classes % 128)))
    block = (layers, node_rows, feat_dim)
    square = (feat_dim, feat_dim)
    vmem = pl.BlockSpec(memory_space=pltpu.VMEM)
    dma = pltpu.SemaphoreType.DMA
    out = pl.pallas_call(
        functools.partial(window_kernel, layers, peers, slots, classes, scale),
        out_shape=(
            jax.ShapeDtypeStruct(block, bf16),
            jax.ShapeDtypeStruct(block, bf16),
            jax.ShapeDtypeStruct(square, f32),
            jax.ShapeDtypeStruct(square, f32),
        ),
        in_specs=[vmem] * 10,
        out_specs=[vmem] * 4,
        scratch_shapes=[
            pltpu.VMEM((layers + 1, node_rows, feat_dim), bf16),
            pltpu.VMEM(block, bf16),
            pltpu.VMEM(block, f32),
            pltpu.VMEM(block, bf16),
            pltpu.VMEM((layers + 1, node_rows, feat_dim), bf16),
            pltpu.VMEM((layers, 2) + square, bf16),
            pltpu.VMEM((ext_rows, feat_dim), bf16),
            pltpu.VMEM((slot_rows, feat_dim), bf16),
            pltpu.VMEM((2 * layers, slot_rows, feat_dim), f32),
            pltpu.VMEM((2 * layers, slot_rows, feat_dim), f32),
            pltpu.VMEM(block, bf16),
            pltpu.VMEM(block, bf16),
            pltpu.VMEM(block, bf16),
            pltpu.VMEM((2,) + square, f32),
            pltpu.VMEM(square, bf16),
            pltpu.VMEM(square, bf16),
            pltpu.VMEM(square, bf16),
            pltpu.VMEM(square, bf16),
            pltpu.VMEM((2,) + square, bf16),
            dma((layers,)), dma((layers,)), dma((layers,)), dma((layers,)),
            dma((2 * layers,)), dma((2 * layers,)),
            dma((5, layers)), dma((5, layers)),
            dma, dma, dma, dma,
            dma, dma((chips,)), dma, dma((chips,)),
        ],
        compiler_params=pltpu.CompilerParams(
            collective_id=0, has_side_effects=True, vmem_limit_bytes=56 * 1024 * 1024
        ),
        cost_estimate=pl.CostEstimate(flops=6 * 10**9, bytes_accessed=10**7, transcendentals=10**6),
    )(
        features, w_self[0], w_neigh[0], w_out,
        pick(labels, me)[:, None], pick(train_mask, me)[:, None],
        adjacency, adjacency.T, selector, selector.T,
    )
    return out[0][None], out[1][None], out[2][None], out[3][None]


def solution(mesh):
    in_specs = (
        P(None, "node", None),
        P("layer", None, None),
        P("layer", None, None),
        P(),
        P(None, "node"),
        P(None, "node"),
        P(None, "node", None, None),
        P(None, "node", None, None, None, None),
        P(None, "node", None, None),
        P(None, "node", None),
    )
    out_specs = (
        P("layer", None, "node", None),
        P("layer", None, "node", None),
        P("layer", None, None),
        P("layer", None, None),
    )
    return jax.shard_map(body, mesh=mesh, in_specs=in_specs, out_specs=out_specs, check_vma=False)
```

time: 332 us -> 135 us (0.41); the launches traced: 326 us -> 135 us
  waiting for transfers between devices: 184 us -> 0 us
  Pallas kernels: 0 us -> 118 us
  starting transfers between devices: 62.8 us -> 0 us
  matrix products: 42.2 us -> 0 us
  between operations: 14.1 us -> 0.72 us
  other arithmetic: 13.6 us -> 2 us
  local copies, waits for them, and re-layouts: 9.73 us -> 13.9 us
    pallas_call x0 -> x1, Pallas kernels: none -> 118 us  [body(): pl.pallas_call(functools.partial(window_kernel, layers, peers, slots, cla...]
    all_to_all x11 -> x0, waiting for transfers between devices: 71.3 us -> none  [the longest x1 44 us: body(): lax.all_to_all(jnp.stack(weight_grads), 'layer', split_axis=0, concat_axi...]
    all_to_all x11 -> x0, starting transfers between devices: 62.6 us -> none  [the longest x8 50.7 us: swap_rows(): lax.all_to_all(parts, 'node', split_axis=0, concat_axis=0, tiled=True)]
    all_gather x2 -> x0, waiting for transfers between devices: 61.5 us -> none  [the longest x1 35.8 us: body(): weights_neigh = lax.all_gather(w_neigh[0], 'layer')]
    psum x1 -> x0, waiting for transfers between devices: 49.5 us -> none  [body(): total = lax.psum(mine, 'node').astype(jnp.float32) * scale]
    dot_general x38 -> x0, matrix products: 42.2 us -> none  [dot(): lax.dot_general(a, b, (dims, ((), ())), preferred_element_type=jnp.float32)]
    another operation x3 -> x0, other arithmetic: 5.86 us -> none  [the longest x1 3.65 us: body(): jnp.stack(weight_grads)]
    unnamed x27 -> x16, local copies, waits for them, and re-layouts: 2.64 us -> 7.62 us
  transfers between devices with their start and end apart: 14 -> 0, of which waited for: 13 -> 0; matrix products, arithmetic and copies ran while one was open for 8% -> 0% of each run, Pallas kernels for 0% -> 0%
where the time goes in v2:
time: 135 us
  Pallas kernels  118 us (87%)
  local copies, waits for them, and re-layouts  13.9 us (10%)
  other arithmetic  2 us (1%)
    pallas_call x1, Pallas kernels, body(): pl.pallas_call(functools.partial(window_kernel, layers, peers, slots, cla...  118 us
    unnamed x16, local copies, waits for them, and re-layouts  7.62 us

profile of v2, /device:TPU:25, one launch (start us, length us, event | category | flops | bytes accessed | tf_op | source)
XLA Modules:
  0.0 134.7 jit_solution(8652257147906391473)
XLA Ops:
  0.7 0.7 fusion.5
  1.3 0.1 iota_compare_fusion.1
  1.4 0.1 lt.40
  1.5 0.7 fusion.4
  2.2 0.1 iota_compare_fusion.2
  2.2 0.7 fusion.2
  3.0 0.1 eq.39
  3.1 0.6 fusion.1
  3.7 0.7 copy.27.sel
  4.4 0.8 copy.24.labels
  5.2 0.8 copy.25.mask
  6.0 1.1 copy.22
  7.1 0.7 pad.10.w_out
  7.8 1.0 bitcast_convert_fusion
  8.8 0.2 select_reduce_fusion
  9.0 0.2 copy.23
  9.2 0.8 copy.26.adj
  10.1 118.1 %shard_map.129 = (bf16[4,256,512]{2,1,0:T(8,128)(2,1)}, bf16[4,256,512]{2,1,0:T(8,128)(2,1)}, f32[512,512]{1,0:T(8,128)}, f32[512,512]{1,0:T(8,128)}) custom-call(bf16[4,256,512]{2,1,0:T(8,128)(2,1)} %feats.1, bf16[512,512]{1,0:T(8,128)(2,1)} %bitcast.44, bf16[512,512]{1,0:T(8,128)(2,1)} %bitcast.45, bf16[512,256]{1,0:T(8,128)(2,1)} %pad.10.w_out, ...), custom_call_target="tpu_custom_call" | custom-call | flops 6000000000 | bytes 10000000 | tf_op jit(solution)/shard_map/pallas_call | solution.py:284
  128.2 2.4 %copy.37 = bf16[1,4,256,512]{3,2,1,0:T(8,128)(2,1)} copy(bf16[1,4,256,512]{3,2,1,0:T(8,128)(2,1)} %bitcast.39) | data formatting | bytes 2097152
  130.6 1.0 copy.38
  131.5 0.6 copy-done.2
  132.2 1.0 copy.39
  133.1 0.6 copy-done.1
  133.8 1.0 copy.40
  (11 shorter events, 0.1 us)
Async XLA Ops:
  0.6 2.3 %copy-start = (s32[4,1,8,8]{3,2,1,0:T(8,128)S(1)}, s32[4,1,8,8]{3,2,1,0:T(8,128)}, u32[]{:S(2)}) copy-start(s32[4,1,8,8]{3,2,1,0:T(8,128)} %param.18) | copy-start | bytes 3076
  9.2 0.8 copy-start.4
  128.2 2.4 %copy-start.3 = (bf16[4,256,512]{2,1,0:T(8,128)(2,1)S(1)}, bf16[4,256,512]{2,1,0:T(8,128)(2,1)}, u32[]{:S(2)}) copy-start(bf16[4,256,512]{2,1,0:T(8,128)(2,1)} %get-tuple-element.9) | copy-start | bytes 3145732
  130.6 1.6 %copy-start.2 = (f32[512,512]{1,0:T(8,128)S(1)}, f32[512,512]{1,0:T(8,128)}, u32[]{:S(2)}) copy-start(f32[512,512]{1,0:T(8,128)} %get-tuple-element.10) | copy-start | bytes 3145732
  132.2 1.6 %copy-start.1 = (f32[512,512]{1,0:T(8,128)S(1)}, f32[512,512]{1,0:T(8,128)}, u32[]{:S(2)}) copy-start(f32[512,512]{1,0:T(8,128)} %get-tuple-element.11) | copy-start | bytes 3145732

commit v3 on v2

--- a/solution.py
+++ b/solution.py
@@ -8,37 +8,20 @@
 from jax.sharding import PartitionSpec as P
 
 
-def pick(array, index):
-    return lax.dynamic_index_in_dim(array, index, 0, keepdims=False)
-
-
 def dot(a, b, dims=((1,), (0,))):
     return lax.dot_general(a, b, (dims, ((), ())), preferred_element_type=jnp.float32)
 
 
-def dense_tiles(col_tiles, values, col_count):
-    row_tiles, degree, tile, _ = values.shape
-    chosen = col_tiles[:, :, None] == jnp.arange(col_count)[None, None, :]
-    wide = jnp.where(chosen[:, :, :, None, None], values[:, :, None].astype(jnp.float32), 0.0)
-    return jnp.sum(wide, axis=1).transpose(0, 2, 1, 3).reshape(row_tiles * tile, col_count * tile).astype(jnp.bfloat16)
-
-
-def slot_selector(send_list, counts, node_rows):
-    peers, slots = send_list.shape
-    live = jnp.arange(slots)[None, :] < counts[:, None]
-    hit = send_list[:, :, None] == jnp.arange(node_rows)[None, None, :]
-    return (hit & live[:, :, None]).astype(jnp.bfloat16).reshape(peers * slots, node_rows)
-
-
 MESH = pl.DeviceIdType.MESH
 
 
 def window_kernel(
-    layers, peers, slots, classes, scale,
-    feats, w_self, w_neigh, w_out, labels, mask, adj, adj_t, sel, sel_t,
-    acts_out, grads_out, gself_out, gneigh_out,
+    layers, peers, slots, classes,
+    feats, w_self, w_neigh, w_out, labels, mask, cols, vals, rows,
+    acts_out, grads_out, final,
+    adj, adj_t, sel, sel_t,
     hid, agg, pre, dpre, dout, wts, ext, back, outbox, inbox, rec_hid, rec_agg, rec_dpre,
-    gsum, gsend, gsib, chip, parts, final,
+    gsum, gsend, gsib, chip, parts,
     w_send, w_recv, f_send, f_recv, x_send, x_recv, blk_send, blk_recv,
     sib_send, sib_recv, rs_send, rs_recv, ag_send, ag_recv, fw_send, fw_recv,
 ):
@@ -78,8 +61,8 @@
     barrier = pltpu.get_barrier_semaphore()
     other_layers(lambda i: pl.semaphore_signal(barrier, inc=1, device_id=(i, node), device_id_type=MESH))
     other_nodes(lambda i: pl.semaphore_signal(barrier, inc=1, device_id=(me, i), device_id_type=MESH))
-    wts[me, 0] = w_self[...]
-    wts[me, 1] = w_neigh[...]
+    wts[me, 0] = w_self[0]
+    wts[me, 1] = w_neigh[0]
     pl.semaphore_wait(barrier, layers - 1 + peers - 1)
 
     def send_weights(i):
@@ -90,6 +73,18 @@
     hid[0] = feats[me]
     ext[...] = jnp.zeros_like(ext)
     back[...] = jnp.zeros_like(back)
+    _, _, row_tiles, degree, tile, _ = vals.shape
+    for r in range(row_tiles):
+        for c in range(adj.shape[1] // tile):
+            block = jnp.zeros((tile, tile), f32)
+            for j in range(degree):
+                block = block + vals[me, 0, r, j].astype(f32) * jnp.where(cols[me, 0, r, j] == c, 1.0, 0.0)
+            adj[r * tile : (r + 1) * tile, c * tile : (c + 1) * tile] = block.astype(bf16)
+            adj_t[c * tile : (c + 1) * tile, r * tile : (r + 1) * tile] = jnp.transpose(block).astype(bf16)
+    hits = lax.broadcasted_iota(jnp.int32, sel_t.shape, 0) == rows[pl.ds(me, 1), :]
+    hits = jnp.where(hits, 1.0, 0.0)
+    sel_t[...] = hits.astype(bf16)
+    sel[...] = jnp.transpose(hits).astype(bf16)
 
     @pl.when(me == 0)
     def _():
@@ -153,8 +148,12 @@
     real = lax.broadcasted_iota(jnp.int32, logits.shape, 1)
     expo = jnp.where(real < classes, jnp.exp(logits), 0.0)
     probs = expo / jnp.sum(expo, axis=-1, keepdims=True)
-    onehot = (labels[...] == real).astype(f32)
-    g_logits = (mask[...].astype(f32) * (probs - onehot)).astype(bf16)
+    wide = (logits.shape[1], node_rows)
+    onehot = jnp.transpose(
+        jnp.where(lax.broadcasted_iota(jnp.int32, wide, 0) == labels[pl.ds(me, 1), :], 1.0, 0.0)
+    )
+    trained = jnp.transpose(jnp.broadcast_to(mask[pl.ds(me, 1), :].astype(f32), wide))
+    g_logits = (trained * (probs - onehot)).astype(bf16)
     dout[layers] = dot(g_logits, w_out[...], ((1,), (1,))).astype(bf16)
 
     def backward(turn):
@@ -233,8 +232,6 @@
 
     other_chips(take_final)
     each(chips, lambda i: drain(final.at[1 - core, rows_of(i)], fw_recv.at[i]))
-    gself_out[...] = final[0].astype(f32) * scale
-    gneigh_out[...] = final[1].astype(f32) * scale
 
     def finish_layer(i):
         drain(acts_out.at[i], blk_recv.at[1, i])
@@ -259,7 +256,6 @@
 
 
 def body(features, w_self, w_neigh, w_out, labels, train_mask, tile_cols, tile_vals, send_rows, send_counts):
-    me = lax.axis_index("layer")
     layers = lax.axis_size("layer")
     peers = lax.axis_size("node")
     spans, node_rows, feat_dim = features.shape
@@ -273,25 +269,28 @@
     scale = 1.0 / (spans * node_rows * peers)
     f32, bf16 = jnp.float32, jnp.bfloat16
 
-    adjacency = dense_tiles(pick(tile_cols, me)[0], pick(tile_vals, me)[0], ext_rows // tile)
-    selector = slot_selector(pick(send_rows, me)[0], pick(send_counts, me)[0], node_rows)
-    selector = jnp.pad(selector, ((0, slot_rows - peers * slots), (0, 0)))
+    live = jnp.arange(slots) < send_counts[:, 0, :, None]
+    slot_of = jnp.where(live, send_rows[:, 0], -1).reshape(spans, peers * slots)
+    slot_of = jnp.pad(slot_of, ((0, 0), (0, slot_rows - peers * slots)), constant_values=-1)
     w_out = jnp.pad(w_out, ((0, 0), (0, -classes % 128)))
     block = (layers, node_rows, feat_dim)
     square = (feat_dim, feat_dim)
     vmem = pl.BlockSpec(memory_space=pltpu.VMEM)
     dma = pltpu.SemaphoreType.DMA
     out = pl.pallas_call(
-        functools.partial(window_kernel, layers, peers, slots, classes, scale),
+        functools.partial(window_kernel, layers, peers, slots, classes),
         out_shape=(
             jax.ShapeDtypeStruct(block, bf16),
             jax.ShapeDtypeStruct(block, bf16),
-            jax.ShapeDtypeStruct(square, f32),
-            jax.ShapeDtypeStruct(square, f32),
+            jax.ShapeDtypeStruct((2,) + square, bf16),
         ),
-        in_specs=[vmem] * 10,
-        out_specs=[vmem] * 4,
+        in_specs=[vmem] * 6 + [pl.BlockSpec(memory_space=pltpu.SMEM)] + [vmem] * 2,
+        out_specs=[vmem] * 3,
         scratch_shapes=[
+            pltpu.VMEM((node_rows, ext_rows), bf16),
+            pltpu.VMEM((ext_rows, node_rows), bf16),
+            pltpu.VMEM((slot_rows, node_rows), bf16),
+            pltpu.VMEM((node_rows, slot_rows), bf16),
             pltpu.VMEM((layers + 1, node_rows, feat_dim), bf16),
             pltpu.VMEM(block, bf16),
             pltpu.VMEM(block, f32),
@@ -310,7 +309,6 @@
             pltpu.VMEM(square, bf16),
             pltpu.VMEM(square, bf16),
             pltpu.VMEM(square, bf16),
-            pltpu.VMEM((2,) + square, bf16),
             dma((layers,)), dma((layers,)), dma((layers,)), dma((layers,)),
             dma((2 * layers,)), dma((2 * layers,)),
             dma((5, layers)), dma((5, layers)),
@@ -322,11 +320,9 @@
         ),
         cost_estimate=pl.CostEstimate(flops=6 * 10**9, bytes_accessed=10**7, transcendentals=10**6),
     )(
-        features, w_self[0], w_neigh[0], w_out,
-        pick(labels, me)[:, None], pick(train_mask, me)[:, None],
-        adjacency, adjacency.T, selector, selector.T,
+        features, w_self, w_neigh, w_out, labels, train_mask, tile_cols, tile_vals, slot_of,
     )
-    return out[0][None], out[1][None], out[2][None], out[3][None]
+    return out[0][None], out[1][None], out[2][:1].astype(f32) * scale, out[2][1:].astype(f32) * scale
 
 
 def solution(mesh):

time: 135 us -> 128 us (0.948)
  local copies, waits for them, and re-layouts: 13.9 us -> 6.59 us
    unnamed x16 -> x9, local copies, waits for them, and re-layouts: 7.62 us -> 4.22 us
    mul x0 -> x1, other arithmetic: none -> 2.9 us  [body(): out[2][1:].astype(f32) * scale]
    broadcast_in_dim x3 -> x0, local copies, waits for them, and re-layouts: 2.29 us -> none  [the longest x2 1.51 us: body(): pick(labels, me)[:, None]]
where the time goes in v3:
time: 128 us
  Pallas kernels  118 us (92%)
  local copies, waits for them, and re-layouts  6.59 us (5%)
  other arithmetic  2.9 us (2%)
    pallas_call x1, Pallas kernels, body(): pl.pallas_call(functools.partial(window_kernel, layers, peers, slots, cla...  118 us
    unnamed x9, local copies, waits for them, and re-layouts  4.22 us
    mul x1, other arithmetic, body(): out[2][1:].astype(f32) * scale  2.9 us

profile of v3, /device:TPU:25, one launch (start us, length us, event | category | flops | bytes accessed | tf_op | source)
XLA Modules:
  0.0 127.9 jit_solution(14611835466152553002)
XLA Ops:
  0.6 0.8 squeeze.3
  1.4 0.0 copy-start.2
  1.4 0.1 lt.23
  1.5 0.6 copy-done.2
  2.1 0.1 lt.26
  2.2 0.1 lt.27
  2.3 0.6 pad.9.rows
  2.9 1.1 copy.14
  3.9 0.7 pad.8.w_out
  4.7 117.7 %shard_map.129 = (bf16[4,256,512]{2,1,0:T(8,128)(2,1)}, bf16[4,256,512]{2,1,0:T(8,128)(2,1)}, bf16[2,512,512]{2,1,0:T(8,128)(2,1)}) custom-call(bf16[4,256,512]{2,1,0:T(8,128)(2,1)} %feats.1, bf16[1,512,512]{2,1,0:T(8,128)(2,1)} %w_self.1, bf16[1,512,512]{2,1,0:T(8,128)(2,1)} %w_neigh.1, bf16[512,256]{1,0:T(8,128)(2,1)} %pad.8.w_out, s32[4,256]{1,0:T(4,128)} %labels.1, ...), custom_call_target="tpu_custom_call" | custom-call | flops 6000000000 | bytes 10000000 | tf_op jit(solution)/shard_map/pallas_call | solution.py:280
  122.4 0.0 copy-start.1
  122.4 2.9 %convert_multiply_fusion = (f32[1,512,512]{2,1,0:T(8,128)}, f32[1,512,512]{2,1,0:T(8,128)}) fusion(bf16[2,512,512]{2,1,0:T(8,128)(2,1)} %get-tuple-element.9), kind=kLoop, calls=%fused_computation | loop fusion | flops 1048576 | bytes 3145728 | tf_op jit(solution)/shard_map/mul | solution.py:325
  125.3 0.0 copy-done.1
  125.3 0.0 copy-start
  125.3 1.0 copy.17
  126.3 0.6 copy-done
  126.9 1.0 copy.18
  (2 shorter events, 0.0 us)
Async XLA Ops:
  1.4 0.7 copy-start.2
  122.4 2.9 %copy-start.1 = (bf16[4,256,512]{2,1,0:T(8,128)(2,1)S(1)}, bf16[4,256,512]{2,1,0:T(8,128)(2,1)}, u32[]{:S(2)}) copy-start(bf16[4,256,512]{2,1,0:T(8,128)(2,1)} %get-tuple-element.7) | copy-start | bytes 3145732
  125.3 1.6 %copy-start = (bf16[4,256,512]{2,1,0:T(8,128)(2,1)S(1)}, bf16[4,256,512]{2,1,0:T(8,128)(2,1)}, u32[]{:S(2)}) copy-start(bf16[4,256,512]{2,1,0:T(8,128)(2,1)} %get-tuple-element.8) | copy-start | bytes 3145732

commit v4 on v3

--- a/solution.py
+++ b/solution.py
@@ -20,7 +20,7 @@
     feats, w_self, w_neigh, w_out, labels, mask, cols, vals, rows,
     acts_out, grads_out, final,
     adj, adj_t, sel, sel_t,
-    hid, agg, pre, dpre, dout, wts, ext, back, outbox, inbox, rec_hid, rec_agg, rec_dpre,
+    hid, agg, pre, dpre, dout, wts, ext, back, outbox, inbox, rec, rec_dpre,
     gsum, gsend, gsib, chip, parts,
     w_send, w_recv, f_send, f_recv, x_send, x_recv, blk_send, blk_recv,
     sib_send, sib_recv, rs_send, rs_recv, ag_send, ag_recv, fw_send, fw_recv,
@@ -88,7 +88,7 @@
 
     @pl.when(me == 0)
     def _():
-        rec_hid[...] = feats[...]
+        rec[0] = feats[...]
 
     def swap_start(turn):
         def send(i):
@@ -127,7 +127,7 @@
         ext[node_rows : node_rows + peers * slots] = inbox[layer, : peers * slots].astype(bf16)
         aggregate = dot(adj[...], ext[...]).astype(bf16)
         agg[layer] = aggregate
-        give(0, agg.at[layer], rec_agg, layer)
+        give(0, agg.at[layer], rec.at[1], layer)
 
         @pl.when(layer != me)
         def _():
@@ -140,7 +140,7 @@
 
         @pl.when(layer + 1 < layers)
         def _():
-            give(2, hid.at[layer + 1], rec_hid, lax.rem(layer + 1, layers))
+            give(2, hid.at[layer + 1], rec.at[0], lax.rem(layer + 1, layers))
 
     each(layers, forward)
 
@@ -175,31 +175,26 @@
 
     each(layers, backward)
 
-    gsum[...] = jnp.zeros_like(gsum)
-
-    def add_span(i):
-        span = lax.rem(me + i, layers)
-
-        @pl.when(i != 0)
-        def _():
-            drain(rec_agg.at[span], blk_recv.at[0, span])
-            drain(rec_dpre.at[span], blk_recv.at[3, span])
-
-            @pl.when(me != 0)
-            def _():
-                drain(rec_hid.at[span], blk_recv.at[2, span])
-
-        over_rows = ((0,), (0,))
-        gsum[0] += dot(rec_hid[span], rec_dpre[span], over_rows)
-        gsum[1] += dot(rec_agg[span], rec_dpre[span], over_rows)
-
-    each(layers, add_span)
-
-    gsend[...] = gsum[1 - core].astype(bf16)
+    def take_span(span):
+        drain(rec.at[1, span], blk_recv.at[0, span])
+        drain(rec_dpre.at[span], blk_recv.at[3, span])
+
+        @pl.when(me != 0)
+        def _():
+            drain(rec.at[0, span], blk_recv.at[2, span])
+
+    other_layers(take_span)
+
+    def weight_grad(side):
+        left = rec[side].reshape(layers * node_rows, feat_dim)
+        return dot(left, rec_dpre[...].reshape(layers * node_rows, feat_dim), ((0,), (0,)))
+
+    gsend[...] = weight_grad(1 - core).astype(bf16)
     to_sibling = remote(gsend, gsib, sib_send, sib_recv, (me, sibling))
     to_sibling.start()
+    gsum[...] = weight_grad(core)
     drain(gsib, sib_recv)
-    chip[...] = (gsum[core] + gsib[...].astype(f32)).astype(bf16)
+    chip[...] = (gsum[...] + gsib[...].astype(f32)).astype(bf16)
 
     def rows_of(i):
         return pl.ds(pl.multiple_of(i * chunk, chunk), chunk)
@@ -301,10 +296,9 @@
             pltpu.VMEM((slot_rows, feat_dim), bf16),
             pltpu.VMEM((2 * layers, slot_rows, feat_dim), f32),
             pltpu.VMEM((2 * layers, slot_rows, feat_dim), f32),
+            pltpu.VMEM((2,) + block, bf16),
             pltpu.VMEM(block, bf16),
-            pltpu.VMEM(block, bf16),
-            pltpu.VMEM(block, bf16),
-            pltpu.VMEM((2,) + square, f32),
+            pltpu.VMEM(square, f32),
             pltpu.VMEM(square, bf16),
             pltpu.VMEM(square, bf16),
             pltpu.VMEM(square, bf16),

time: 128 us -> 128 us (level)
  no operation moved by 1% of the time
where the time goes in v4:
time: 128 us
  Pallas kernels  118 us (92%)
  local copies, waits for them, and re-layouts  6.59 us (5%)
  other arithmetic  2.9 us (2%)
    pallas_call x1, Pallas kernels, body(): pl.pallas_call(functools.partial(window_kernel, layers, peers, slots, cla...  118 us
    unnamed x9, local copies, waits for them, and re-layouts  4.22 us
    mul x1, other arithmetic, body(): out[2][1:].astype(f32) * scale  2.9 us

profile of v4, /device:TPU:25, one launch (start us, length us, event | category | flops | bytes accessed | tf_op | source)
XLA Modules:
  0.0 127.7 jit_solution(14497431353422899223)
XLA Ops:
  0.6 0.8 squeeze.3
  1.4 0.0 copy-start.2
  1.4 0.1 lt.23
  1.5 0.6 copy-done.2
  2.1 0.1 lt.26
  2.2 0.1 lt.27
  2.3 0.6 pad.9.rows
  2.9 1.1 copy.14
  3.9 0.7 pad.8.w_out
  4.7 117.5 %shard_map.129 = (bf16[4,256,512]{2,1,0:T(8,128)(2,1)}, bf16[4,256,512]{2,1,0:T(8,128)(2,1)}, bf16[2,512,512]{2,1,0:T(8,128)(2,1)}) custom-call(bf16[4,256,512]{2,1,0:T(8,128)(2,1)} %feats.1, bf16[1,512,512]{2,1,0:T(8,128)(2,1)} %w_self.1, bf16[1,512,512]{2,1,0:T(8,128)(2,1)} %w_neigh.1, bf16[512,256]{1,0:T(8,128)(2,1)} %pad.8.w_out, s32[4,256]{1,0:T(4,128)} %labels.1, ...), custom_call_target="tpu_custom_call" | custom-call | flops 6000000000 | bytes 10000000 | tf_op jit(solution)/shard_map/pallas_call | solution.py:275
  122.2 0.0 copy-start.1
  122.2 2.9 %convert_multiply_fusion = (f32[1,512,512]{2,1,0:T(8,128)}, f32[1,512,512]{2,1,0:T(8,128)}) fusion(bf16[2,512,512]{2,1,0:T(8,128)(2,1)} %get-tuple-element.9), kind=kLoop, calls=%fused_computation | loop fusion | flops 1048576 | bytes 3145728 | tf_op jit(solution)/shard_map/mul | solution.py:319
  125.1 0.0 copy-done.1
  125.1 0.0 copy-start
  125.1 1.0 copy.17
  126.1 0.6 copy-done
  126.7 1.0 copy.18
  (2 shorter events, 0.0 us)
Async XLA Ops:
  1.4 0.7 copy-start.2
  122.2 2.9 %copy-start.1 = (bf16[4,256,512]{2,1,0:T(8,128)(2,1)S(1)}, bf16[4,256,512]{2,1,0:T(8,128)(2,1)}, u32[]{:S(2)}) copy-start(bf16[4,256,512]{2,1,0:T(8,128)(2,1)} %get-tuple-element.7) | copy-start | bytes 3145732
  125.1 1.6 %copy-start = (bf16[4,256,512]{2,1,0:T(8,128)(2,1)S(1)}, bf16[4,256,512]{2,1,0:T(8,128)(2,1)}, u32[]{:S(2)}) copy-start(bf16[4,256,512]{2,1,0:T(8,128)(2,1)} %get-tuple-element.8) | copy-start | bytes 3145732

commit v5 on v3

--- a/solution.py
+++ b/solution.py
@@ -113,6 +113,10 @@
         def _():
             remote(src, dst.at[me], blk_send.at[kind, owner], blk_recv.at[kind, me], (owner, node)).start()
 
+    def slope(preact):
+        sigma = jax.nn.sigmoid(preact)
+        return sigma * (1.0 + preact * (1.0 - sigma))
+
     def forward(layer):
         outbox[layer] = dot(sel[...], hid[layer])
         swap_start(layer)
@@ -123,17 +127,23 @@
             remote(wts.at[layer, core], wts.at[layer, core], f_send.at[layer], f_recv.at[layer], (me, sibling)).start()
 
         ext[:node_rows] = hid[layer]
+
+        @pl.when(layer > 0)
+        def _():
+            pre[layer - 1] = slope(pre[layer - 1])
+
+        @pl.when(layer != me)
+        def _():
+            drain(wts.at[layer, 1 - core], f_recv.at[layer])
+
+        pre[layer] = dot(hid[layer], wts[layer, 0])
         drain(swap_bytes(layer), x_recv.at[layer])
         ext[node_rows : node_rows + peers * slots] = inbox[layer, : peers * slots].astype(bf16)
         aggregate = dot(adj[...], ext[...]).astype(bf16)
         agg[layer] = aggregate
         give(0, agg.at[layer], rec_agg, layer)
 
-        @pl.when(layer != me)
-        def _():
-            drain(wts.at[layer, 1 - core], f_recv.at[layer])
-
-        preact = dot(hid[layer], wts[layer, 0]) + dot(aggregate, wts[layer, 1])
+        preact = pre[layer] + dot(aggregate, wts[layer, 1])
         pre[layer] = preact
         hid[layer + 1] = (preact * jax.nn.sigmoid(preact)).astype(bf16)
         give(1, hid.at[layer + 1], acts_out, layer)
@@ -143,6 +153,7 @@
             give(2, hid.at[layer + 1], rec_hid, lax.rem(layer + 1, layers))
 
     each(layers, forward)
+    pre[layers - 1] = slope(pre[layers - 1])
 
     logits = dot(hid[layers], w_out[...])
     real = lax.broadcasted_iota(jnp.int32, logits.shape, 1)
@@ -158,9 +169,7 @@
 
     def backward(turn):
         layer = layers - 1 - turn
-        preact = pre[layer]
-        sigma = jax.nn.sigmoid(preact)
-        d_pre = (dout[layer + 1].astype(f32) * (sigma * (1.0 + preact * (1.0 - sigma)))).astype(bf16)
+        d_pre = (dout[layer + 1].astype(f32) * pre[layer]).astype(bf16)
         dpre[layer] = d_pre
         d_agg = dot(d_pre, wts[layer, 1], ((1,), (1,))).astype(bf16)
         d_ext = dot(adj_t[...], d_agg)

time: 128 us -> 128 us (level); the launches traced: 128 us -> 125 us
  Pallas kernels: 118 us -> 115 us
    pallas_call x1, Pallas kernels: 118 us -> 115 us  [body(): pl.pallas_call(functools.partial(window_kernel, layers, peers, slots, cla...]
where the time goes in v5:
time: 128 us; the launch traced here: 125 us
  Pallas kernels  115 us (90%)
  local copies, waits for them, and re-layouts  6.59 us (5%)
  other arithmetic  2.9 us (2%)
    pallas_call x1, Pallas kernels, body(): pl.pallas_call(functools.partial(window_kernel, layers, peers, slots, cla...  115 us
    unnamed x9, local copies, waits for them, and re-layouts  4.22 us
    mul x1, other arithmetic, body(): out[2][1:].astype(f32) * scale  2.9 us

profile of v5, /device:TPU:25, one launch (start us, length us, event | category | flops | bytes accessed | tf_op | source)
XLA Modules:
  0.0 125.3 jit_solution(8663202727360087189)
XLA Ops:
  0.6 0.8 squeeze.3
  1.4 0.0 copy-start.2
  1.4 0.1 lt.23
  1.5 0.6 copy-done.2
  2.1 0.1 lt.26
  2.2 0.1 lt.27
  2.3 0.6 pad.9.rows
  2.9 1.1 copy.14
  3.9 0.7 pad.8.w_out
  4.7 115.1 %shard_map.129 = (bf16[4,256,512]{2,1,0:T(8,128)(2,1)}, bf16[4,256,512]{2,1,0:T(8,128)(2,1)}, bf16[2,512,512]{2,1,0:T(8,128)(2,1)}) custom-call(bf16[4,256,512]{2,1,0:T(8,128)(2,1)} %feats.1, bf16[1,512,512]{2,1,0:T(8,128)(2,1)} %w_self.1, bf16[1,512,512]{2,1,0:T(8,128)(2,1)} %w_neigh.1, bf16[512,256]{1,0:T(8,128)(2,1)} %pad.8.w_out, s32[4,256]{1,0:T(4,128)} %labels.1, ...), custom_call_target="tpu_custom_call" | custom-call | flops 6000000000 | bytes 10000000 | tf_op jit(solution)/shard_map/pallas_call | solution.py:289
  119.8 0.0 copy-start.1
  119.8 2.9 %convert_multiply_fusion = (f32[1,512,512]{2,1,0:T(8,128)}, f32[1,512,512]{2,1,0:T(8,128)}) fusion(bf16[2,512,512]{2,1,0:T(8,128)(2,1)} %get-tuple-element.9), kind=kLoop, calls=%fused_computation | loop fusion | flops 1048576 | bytes 3145728 | tf_op jit(solution)/shard_map/mul | solution.py:334
  122.7 0.0 copy-done.1
  122.7 0.0 copy-start
  122.7 1.0 copy.17
  123.7 0.6 copy-done
  124.3 1.0 copy.18
  (2 shorter events, 0.0 us)
Async XLA Ops:
  1.4 0.7 copy-start.2
  119.8 2.9 %copy-start.1 = (bf16[4,256,512]{2,1,0:T(8,128)(2,1)S(1)}, bf16[4,256,512]{2,1,0:T(8,128)(2,1)}, u32[]{:S(2)}) copy-start(bf16[4,256,512]{2,1,0:T(8,128)(2,1)} %get-tuple-element.7) | copy-start | bytes 3145732
  122.7 1.6 %copy-start = (bf16[4,256,512]{2,1,0:T(8,128)(2,1)S(1)}, bf16[4,256,512]{2,1,0:T(8,128)(2,1)}, u32[]{:S(2)}) copy-start(bf16[4,256,512]{2,1,0:T(8,128)(2,1)} %get-tuple-element.8) | copy-start | bytes 3145732
